TPU v7x, 32 devices: a whole 2x2x4 slice. The times are simulated.
32 devices in a mesh: gx: 4 (over y, core), gy: 8 (over z, x).
Axes of the slice: x: 2, y: 2, z: 4, core: 2. Of those that a mesh axis runs over, the one named last changes fastest.
Arguments:
- rhs: float32 [3, 20, 32, 1024], P(None, None, 'gx', 'gy'), may hold values from -6 to 6
- diag_block: bfloat16 [9, 20, 32, 1024], P(None, None, 'gx', 'gy'), may hold values from -0.5625 to 4.75
- mobility: bfloat16 [9, 20, 32, 1024], P(None, None, 'gx', 'gy'), may hold values from -0.34375 to 1.375
- trans: bfloat16 [3, 20, 32, 1024], P(None, None, 'gx', 'gy'), may hold values from 0.5 to 1
- perf_cell: int32 [32, 8, 32], P(('gx', 'gy')), may hold values from 0 to 20479, as said below
- perf_pi: float32 [32, 8, 32], P(('gx', 'gy')), may hold values from 0 to 0.6, as said below
- perf_seg: int32 [32, 8, 32], P(('gx', 'gy')), may hold values from 0 to 255
- seg_parent: int32 [8192], P(('gx', 'gy')), may hold values from -1 to 254, as said below
- seg_trans: float32 [8192], P(('gx', 'gy')), may hold values from 0.5 to 2
- seg_rhs: float32 [8192], P(('gx', 'gy')), may hold values from -6 to 6
Outputs:
- solution: float32 [3, 20, 32, 1024], P(None, None, 'gx', 'gy')
- seg_pressure: float32 [8192], P(('gx', 'gy'))
Inputs may be any that keep to these rules, and one draw needn't show every extreme that they name: `perf_cell`: the 8 slots of a sender-owner pair name consecutive cells along y in one layer and one x column. `perf_pi`: live slots of a sender-owner pair come first among its 8; every sender has one owner with all 8 slots live, and one owner receives all 8 from every sender; some of the owners, drawn from the seed, receive many more than the rest. `seg_parent`: A parent comes just before its segment on the same owner; segment 0 of every owner is at a well head.
All inputs are finite; a program needn't handle non-finite values.
Results may differ from a plain program's by a relative error of at most 0.0003.
Values may be sent and summed in bfloat16 or wider, within the bound.
A program may use at most 128 MiB of HBM per device.

v0:
```python
import jax
import jax.numpy as jnp
from jax import lax
from jax.sharding import PartitionSpec as P

SWEEPS = 4
OUTER = 2


def extended(value, sides, width):
    for axis, dim in sides:
        count, length = (lax.axis_size(axis), value.shape[dim])
        up = [(i, (i + 1) % count) for i in range(count - 1)]
        down = [(j, i) for i, j in up]
        last = lax.slice_in_dim(value, length - width, length, axis=dim)
        leading = lax.slice_in_dim(value, 0, width, axis=dim)
        before = lax.ppermute(last, axis, up)
        after = lax.ppermute(leading, axis, down)
        value = jnp.concatenate([before, value, after], axis=dim)
    return value


def invert_blocks(mat):
    a, b, c, d, e, f, g, h, i = [mat[position] for position in range(9)]
    first = e * i - f * h
    second = f * g - d * i
    third = d * h - e * g
    determinant = a * first + b * second + c * third
    entries = [
        first,
        c * h - b * i,
        b * f - c * e,
        second,
        a * i - c * g,
        c * d - a * f,
        third,
        b * g - a * h,
        a * e - b * d,
    ]
    return jnp.stack([entry / determinant for entry in entries])


def block_apply(mat, vec):
    return jnp.stack(
        [
            mat[3 * row] * vec[0] + mat[3 * row + 1] * vec[1] + mat[3 * row + 2] * vec[2]
            for row in range(3)
        ]
    )


def child_total(values, parent, count):
    return jax.ops.segment_sum(
        jnp.where(parent >= 0, values, 0.0), jnp.maximum(parent, 0), num_segments=count
    )


def on_device(
    rhs, diag_block, mobility, trans, perf_cell, perf_pi, perf_seg, seg_parent, seg_trans, seg_rhs
):
    layers, rows_x, rows_y = (rhs.shape[1], rhs.shape[2], rhs.shape[3])
    dense = diag_block.astype(jnp.float32)
    mob_full = mobility.astype(jnp.float32)
    inverse = invert_blocks(dense)
    trans_f = trans.astype(jnp.float32)
    slots = perf_pi.shape[1]
    owners = perf_pi.shape[2]
    cells_count = layers * rows_x * rows_y
    cell_index = perf_cell[0].reshape(-1)
    weights = perf_pi[0]
    seg_index = perf_seg[0].reshape(-1)
    segments = seg_rhs.shape[0]
    fraction = mob_full[0::3]

    def to_owners(buffer):
        return lax.all_to_all(buffer, ("gx", "gy"), split_axis=1, concat_axis=1, tiled=True)

    weights_in = to_owners(weights)
    seg_diag = seg_trans + child_total(seg_trans, seg_parent, segments)
    seg_diag = seg_diag + jax.ops.segment_sum(
        weights_in.reshape(-1), seg_index, num_segments=segments
    )
    rims = extended(trans[:2], (("gx", 2), ("gy", 3)), 1).astype(jnp.float32)
    x_lower = rims[0, :, :-2, 1:-1] * trans_f[0]
    x_upper = trans_f[0] * rims[0, :, 2:, 1:-1]
    y_lower = rims[1, :, 1:-1, :-2] * trans_f[1]
    y_upper = trans_f[1] * rims[1, :, 1:-1, 2:]
    z_face = trans_f[2, :-1] * trans_f[2, 1:]
    rounds = SWEEPS
    solution = jnp.zeros_like(rhs)
    seg_pressure = jnp.zeros_like(seg_rhs)
    cell_res, seg_res = (rhs, seg_rhs)
    for outer in range(OUTER):
        field, seg_state = (solution, seg_pressure)
        cell_now, seg_now = (cell_res, seg_res)
        for sweep in range(rounds):
            advance_field = field
            advance_seg_state = seg_state
            advance_field = advance_field + block_apply(inverse, cell_now)
            seg_new = advance_seg_state + seg_now / seg_diag
            advance_seg_state = seg_new
            advance_slot_state = lax.all_to_all(
                seg_new[perf_seg[0]], ("gx", "gy"), split_axis=1, concat_axis=1, tiled=True
            )
            flows = weights.reshape(-1) * (
                advance_field[0].reshape(-1)[cell_index] - advance_slot_state.reshape(-1)
            )
            into_cells = (
                jnp.zeros((cells_count,), jnp.float32)
                .at[cell_index]
                .add(flows)
                .reshape(layers, rows_x, rows_y)
            )
            mob_vec = block_apply(mob_full, advance_field)
            rim = extended(mob_vec, (("gx", 2), ("gy", 3)), 1)
            total = x_lower * rim[:, :, :-2, 1:-1] + x_upper * rim[:, :, 2:, 1:-1]
            total = total + y_lower * rim[:, :, 1:-1, :-2] + y_upper * rim[:, :, 1:-1, 2:]
            zeros_layer = jnp.zeros_like(mob_vec[:, :1])
            below = jnp.concatenate([z_face * mob_vec[:, 1:], zeros_layer], axis=1)
            above = jnp.concatenate([zeros_layer, z_face * mob_vec[:, :-1]], axis=1)
            advance_cell_res = (
                rhs
                - block_apply(dense, advance_field)
                + (total + below + above)
                - fraction * into_cells
            )
            arrived = to_owners(flows.reshape(slots, owners))
            upper = jnp.where(seg_parent >= 0, advance_seg_state[jnp.maximum(seg_parent, 0)], 0.0)
            flux = seg_trans * (advance_seg_state - upper)
            into_segs = jax.ops.segment_sum(arrived.reshape(-1), seg_index, num_segments=segments)
            advance_seg_res = seg_rhs - flux + child_total(flux, seg_parent, segments) + into_segs
            field = advance_field
            seg_state = advance_seg_state
            cell_now = advance_cell_res
            seg_now = advance_seg_res
        cell_diff = cell_res - cell_now
        seg_diff = seg_res - seg_now
        local_numer = jnp.sum(cell_res * cell_diff) + jnp.sum(seg_res * seg_diff)
        local_denom = jnp.sum(cell_diff * cell_diff) + jnp.sum(seg_diff * seg_diff)
        numer, denom = lax.psum((local_numer, local_denom), ("gx", "gy"))
        omega = numer / denom
        solution = solution + omega * (field - solution)
        seg_pressure = seg_pressure + omega * (seg_state - seg_pressure)
        cell_res = cell_res - omega * cell_diff
        seg_res = seg_res - omega * seg_diff
    return (solution, seg_pressure)


def solution(mesh):
    return jax.shard_map(
        on_device,
        mesh=mesh,
        in_specs=(
            P(None, None, "gx", "gy"),
            P(None, None, "gx", "gy"),
            P(None, None, "gx", "gy"),
            P(None, None, "gx", "gy"),
            P(("gx", "gy"), None, None),
            P(("gx", "gy"), None, None),
            P(("gx", "gy"), None, None),
            P(("gx", "gy")),
            P(("gx", "gy")),
            P(("gx", "gy")),
        ),
        out_specs=(P(None, None, "gx", "gy"), P(("gx", "gy"))),
        check_vma=False,
    )
```

profile of v0, /device:TPU:0, one launch (start us, length us, event | category | flops | bytes accessed | tf_op | source)
XLA Modules:
  0.0 672.8 jit_solution(1889424020950098371)
XLA Ops:
  11.5 7.3 %all-to-all-start = ((f32[8,32,1]{0,2,1:T(1,128)}), f32[8,32,1]{0,2,1:T(1,128)S(1)}, u32[]{:S(2)}, u32[]{:S(2)}) async-start(f32[8,32,1]{0,2,1:T(1,128)} %copy.13), calls=%async_computation | async-start | bytes 32768 | tf_op jit(solution)/shard_map/all_to_all | solution.py:76
  40.8 5.9 all-to-all-start.1
  77.8 5.4 collective-permute-start.2
  98.6 8.2 %collective-permute-done.7 = f32[3,20,10,1]{3,2,1,0:T(8,128)S(1)} collective-permute-done((f32[3,20,10,1]{3,2,1,0:T(8,128)S(1)}, f32[3,20,10,1]{3,2,1,0:T(8,128)S(1)}, u32[]{:S(2)}, u32[]{:S(2)}) %collective-permute-start.7) | collective-permute-done | bytes 2432 | tf_op jit(solution)/shard_map/ppermute | solution.py:18
  106.8 10.7 %collective-permute-done.6 = f32[3,20,10,1]{3,2,1,0:T(8,128)S(1)} collective-permute-done((f32[3,20,10,1]{3,2,1,0:T(8,128)S(1)}, f32[3,20,10,1]{3,2,1,0:T(8,128)S(1)}, u32[]{:S(2)}, u32[]{:S(2)}) %collective-permute-start.6) | collective-permute-done | bytes 2432 | tf_op jit(solution)/shard_map/ppermute | solution.py:17
  130.1 5.7 all-to-all-start.4
  171.8 10.6 %collective-permute-done.10 = f32[3,20,10,1]{3,2,1,0:T(8,128)} collective-permute-done((f32[3,20,10,1]{3,2,1,0:T(8,128)}, f32[3,20,10,1]{3,2,1,0:T(8,128)}, u32[]{:S(2)}, u32[]{:S(2)}) %collective-permute-start.10) | collective-permute-done | bytes 2432 | tf_op jit(solution)/shard_map/ppermute | solution.py:17
  196.3 5.7 all-to-all-start.6
  238.0 10.6 %collective-permute-done.14 = f32[3,20,10,1]{3,2,1,0:T(8,128)} collective-permute-done((f32[3,20,10,1]{3,2,1,0:T(8,128)}, f32[3,20,10,1]{3,2,1,0:T(8,128)}, u32[]{:S(2)}, u32[]{:S(2)}) %collective-permute-start.14) | collective-permute-done | bytes 2432 | tf_op jit(solution)/shard_map/ppermute | solution.py:17
  265.5 5.8 all-to-all-start.8
  289.8 8.1 %collective-permute-done.19 = f32[3,20,10,1]{3,2,1,0:T(8,128)S(1)} collective-permute-done((f32[3,20,10,1]{3,2,1,0:T(8,128)S(1)}, f32[3,20,10,1]{3,2,1,0:T(8,128)S(1)}, u32[]{:S(2)}, u32[]{:S(2)}) %collective-permute-start.19) | collective-permute-done | bytes 2432 | tf_op jit(solution)/shard_map/ppermute | solution.py:18
  297.9 9.6 %collective-permute-done.18 = f32[3,20,10,1]{3,2,1,0:T(8,128)S(1)} collective-permute-done((f32[3,20,10,1]{3,2,1,0:T(8,128)S(1)}, f32[3,20,10,1]{3,2,1,0:T(8,128)S(1)}, u32[]{:S(2)}, u32[]{:S(2)}) %collective-permute-start.18) | collective-permute-done | bytes 2432 | tf_op jit(solution)/shard_map/ppermute | solution.py:17
  312.8 39.5 %all-reduce.17 = (f32[]{:T(128)}, f32[]{:T(128)}) all-reduce(f32[]{:T(128)S(6)} %add.1196, f32[]{:T(128)S(6)} %add.1197), channel_id=1, replica_groups=mesh['gx'=4,'gy'=8] {'gx','gy'}, use_global_device_ids=true, to_apply=%region_16.17 | all-reduce | flops 2 | bytes 16 | tf_op jit(solution)/shard_map/psum | solution.py:140
  384.7 5.5 all-to-all-start.10
  426.2 10.6 %collective-permute-done.22 = f32[3,20,10,1]{3,2,1,0:T(8,128)} collective-permute-done((f32[3,20,10,1]{3,2,1,0:T(8,128)}, f32[3,20,10,1]{3,2,1,0:T(8,128)}, u32[]{:S(2)}, u32[]{:S(2)}) %collective-permute-start.22) | collective-permute-done | bytes 2432 | tf_op jit(solution)/shard_map/ppermute | solution.py:17
  451.7 5.7 all-to-all-start.12
  493.7 10.6 %collective-permute-done.26 = f32[3,20,10,1]{3,2,1,0:T(8,128)} collective-permute-done((f32[3,20,10,1]{3,2,1,0:T(8,128)}, f32[3,20,10,1]{3,2,1,0:T(8,128)}, u32[]{:S(2)}, u32[]{:S(2)}) %collective-permute-start.26) | collective-permute-done | bytes 2432 | tf_op jit(solution)/shard_map/ppermute | solution.py:17
  519.1 5.7 all-to-all-start.14
  555.4 5.5 collective-permute-done.31
  560.9 10.6 %collective-permute-done.30 = f32[3,20,10,1]{3,2,1,0:T(8,128)} collective-permute-done((f32[3,20,10,1]{3,2,1,0:T(8,128)}, f32[3,20,10,1]{3,2,1,0:T(8,128)}, u32[]{:S(2)}, u32[]{:S(2)}) %collective-permute-start.30) | collective-permute-done | bytes 2432 | tf_op jit(solution)/shard_map/ppermute | solution.py:17
  584.6 6.0 all-to-all-start.16
  607.4 8.3 %collective-permute-done.35 = f32[3,20,10,1]{3,2,1,0:T(8,128)S(1)} collective-permute-done((f32[3,20,10,1]{3,2,1,0:T(8,128)S(1)}, f32[3,20,10,1]{3,2,1,0:T(8,128)S(1)}, u32[]{:S(2)}, u32[]{:S(2)}) %collective-permute-start.35) | collective-permute-done | bytes 2432 | tf_op jit(solution)/shard_map/ppermute | solution.py:18
  615.6 9.6 %collective-permute-done.34 = f32[3,20,10,1]{3,2,1,0:T(8,128)S(1)} collective-permute-done((f32[3,20,10,1]{3,2,1,0:T(8,128)S(1)}, f32[3,20,10,1]{3,2,1,0:T(8,128)S(1)}, u32[]{:S(2)}, u32[]{:S(2)}) %collective-permute-start.34) | collective-permute-done | bytes 2432 | tf_op jit(solution)/shard_map/ppermute | solution.py:17
  629.2 39.3 %all-reduce.16 = (f32[]{:T(128)}, f32[]{:T(128)}) all-reduce(f32[]{:T(128)S(6)} %add.1306, f32[]{:T(128)S(6)} %add.1307), channel_id=1, replica_groups=mesh['gx'=4,'gy'=8] {'gx','gy'}, use_global_device_ids=true, to_apply=%region_34.35 | all-reduce | flops 2 | bytes 16 | tf_op jit(solution)/shard_map/psum | solution.py:140
  (703 shorter events, 410.6 us)
Async XLA Ops:
  5.8 84.1 %collective-permute-start.5 = (f32[3,20,1,128]{3,2,1,0:T(1,128)}, f32[3,20,1,128]{3,2,1,0:T(1,128)}, u32[]{:S(2)}, u32[]{:S(2)}) collective-permute-start(f32[3,20,1,128]{3,2,1,0:T(1,128)} %get-tuple-element.166), channel_id=1, source_target_pairs={{8,0},{16,8},{24,16},{9,1},{17,9},{25,17},{10,2},{18,10},{26,18},{... | collective-permute-start | bytes 92168 | tf_op jit(solution)/shard_map/ppermute | solution.py:18
  7.2 82.6 %collective-permute-start.4 = (f32[3,20,1,128]{3,2,1,0:T(1,128)}, f32[3,20,1,128]{3,2,1,0:T(1,128)}, u32[]{:S(2)}, u32[]{:S(2)}) collective-permute-start(f32[3,20,1,128]{3,2,1,0:T(1,128)} %get-tuple-element.165), channel_id=1, source_target_pairs={{0,8},{8,16},{16,24},{1,9},{9,17},{17,25},{2,10},{10,18},{18,26},{... | collective-permute-start | bytes 92168 | tf_op jit(solution)/shard_map/ppermute | solution.py:17
  11.5 24.0 %all-to-all-start = ((f32[8,32,1]{0,2,1:T(1,128)}), f32[8,32,1]{0,2,1:T(1,128)S(1)}, u32[]{:S(2)}, u32[]{:S(2)}) async-start(f32[8,32,1]{0,2,1:T(1,128)} %copy.13), calls=%async_computation | async-start | bytes 32768 | tf_op jit(solution)/shard_map/all_to_all | solution.py:76
  20.4 54.7 %collective-permute-start.1 = (bf16[2,20,1,128]{3,2,1,0:T(2,128)(2,1)}, bf16[2,20,1,128]{3,2,1,0:T(2,128)(2,1)S(1)}, u32[]{:S(2)}, u32[]{:S(2)}) collective-permute-start(bf16[2,20,1,128]{3,2,1,0:T(2,128)(2,1)} %get-tuple-element.170), channel_id=1, source_target_pairs={{8,0},{16,8},{24,16},{9,1},{17,9},{25,17},{10,2},{18,10},{26,18},{... | collective-permute-start | bytes 30728 | tf_op jit(solution)/shard_map/ppermute | solution.py:18
  21.7 53.4 %collective-permute-start = (bf16[2,20,1,128]{3,2,1,0:T(2,128)(2,1)}, bf16[2,20,1,128]{3,2,1,0:T(2,128)(2,1)S(1)}, u32[]{:S(2)}, u32[]{:S(2)}) collective-permute-start(bf16[2,20,1,128]{3,2,1,0:T(2,128)(2,1)} %get-tuple-element.169), channel_id=1, source_target_pairs={{0,8},{8,16},{16,24},{1,9},{9,17},{17,25},{2,10},{10,18},{18,26},{... | collective-permute-start | bytes 30728 | tf_op jit(solution)/shard_map/ppermute | solution.py:17
  92.3 25.1 %collective-permute-start.6 = (f32[3,20,10,1]{3,2,1,0:T(8,128)S(1)}, f32[3,20,10,1]{3,2,1,0:T(8,128)S(1)}, u32[]{:S(2)}, u32[]{:S(2)}) collective-permute-start(f32[3,20,10,1]{3,2,1,0:T(8,128)S(1)} %get-tuple-element.102), channel_id=1, source_target_pairs={{0,1},{1,2},{2,3},{3,4},{4,5},{5,6},{6,7},{8,9},{9,10},{10,11},{11... | collective-permute-start | bytes 7208 | tf_op jit(solution)/shard_map/ppermute | solution.py:17
  120.5 33.7 %collective-permute-start.9 = (f32[3,20,1,128]{3,2,1,0:T(1,128)}, f32[3,20,1,128]{3,2,1,0:T(1,128)}, u32[]{:S(2)}, u32[]{:S(2)}) collective-permute-start(f32[3,20,1,128]{3,2,1,0:T(1,128)} %get-tuple-element.158), channel_id=1, source_target_pairs={{8,0},{16,8},{24,16},{9,1},{17,9},{25,17},{10,2},{18,10},{26,18},{... | collective-permute-start | bytes 92168 | tf_op jit(solution)/shard_map/ppermute | solution.py:18
  121.8 32.5 %collective-permute-start.8 = (f32[3,20,1,128]{3,2,1,0:T(1,128)}, f32[3,20,1,128]{3,2,1,0:T(1,128)}, u32[]{:S(2)}, u32[]{:S(2)}) collective-permute-start(f32[3,20,1,128]{3,2,1,0:T(1,128)} %get-tuple-element.157), channel_id=1, source_target_pairs={{0,8},{8,16},{16,24},{1,9},{9,17},{17,25},{2,10},{10,18},{18,26},{... | collective-permute-start | bytes 92168 | tf_op jit(solution)/shard_map/ppermute | solution.py:17
  157.7 24.7 %collective-permute-start.10 = (f32[3,20,10,1]{3,2,1,0:T(8,128)}, f32[3,20,10,1]{3,2,1,0:T(8,128)}, u32[]{:S(2)}, u32[]{:S(2)}) collective-permute-start(f32[3,20,10,1]{3,2,1,0:T(8,128)} %get-tuple-element.100), channel_id=1, source_target_pairs={{0,1},{1,2},{2,3},{3,4},{4,5},{5,6},{6,7},{8,9},{9,10},{10,11},{11... | collective-permute-start | bytes 7208 | tf_op jit(solution)/shard_map/ppermute | solution.py:17
  186.8 33.5 %collective-permute-start.13 = (f32[3,20,1,128]{3,2,1,0:T(1,128)}, f32[3,20,1,128]{3,2,1,0:T(1,128)}, u32[]{:S(2)}, u32[]{:S(2)}) collective-permute-start(f32[3,20,1,128]{3,2,1,0:T(1,128)} %get-tuple-element.152), channel_id=1, source_target_pairs={{8,0},{16,8},{24,16},{9,1},{17,9},{25,17},{10,2},{18,10},{26,18},{... | collective-permute-start | bytes 92168 | tf_op jit(solution)/shard_map/ppermute | solution.py:18
  188.1 32.3 %collective-permute-start.12 = (f32[3,20,1,128]{3,2,1,0:T(1,128)}, f32[3,20,1,128]{3,2,1,0:T(1,128)}, u32[]{:S(2)}, u32[]{:S(2)}) collective-permute-start(f32[3,20,1,128]{3,2,1,0:T(1,128)} %get-tuple-element.151), channel_id=1, source_target_pairs={{0,8},{8,16},{16,24},{1,9},{9,17},{17,25},{2,10},{10,18},{18,26},{... | collective-permute-start | bytes 92168 | tf_op jit(solution)/shard_map/ppermute | solution.py:17
  223.9 24.7 %collective-permute-start.14 = (f32[3,20,10,1]{3,2,1,0:T(8,128)}, f32[3,20,10,1]{3,2,1,0:T(8,128)}, u32[]{:S(2)}, u32[]{:S(2)}) collective-permute-start(f32[3,20,10,1]{3,2,1,0:T(8,128)} %get-tuple-element.98), channel_id=1, source_target_pairs={{0,1},{1,2},{2,3},{3,4},{4,5},{5,6},{6,7},{8,9},{9,10},{10,11},{11... | collective-permute-start | bytes 7208 | tf_op jit(solution)/shard_map/ppermute | solution.py:17
  258.3 23.4 %collective-permute-start.17 = (f32[3,20,1,128]{3,2,1,0:T(1,128)}, f32[3,20,1,128]{3,2,1,0:T(1,128)}, u32[]{:S(2)}, u32[]{:S(2)}) collective-permute-start(f32[3,20,1,128]{3,2,1,0:T(1,128)} %get-tuple-element.146), channel_id=1, source_target_pairs={{8,0},{16,8},{24,16},{9,1},{17,9},{25,17},{10,2},{18,10},{26,18},{... | collective-permute-start | bytes 92168 | tf_op jit(solution)/shard_map/ppermute | solution.py:18
  284.5 23.0 %collective-permute-start.18 = (f32[3,20,10,1]{3,2,1,0:T(8,128)S(1)}, f32[3,20,10,1]{3,2,1,0:T(8,128)S(1)}, u32[]{:S(2)}, u32[]{:S(2)}) collective-permute-start(f32[3,20,10,1]{3,2,1,0:T(8,128)S(1)} %get-tuple-element.96), channel_id=1, source_target_pairs={{0,1},{1,2},{2,3},{3,4},{4,5},{5,6},{6,7},{8,9},{9,10},{10,11},{11... | collective-permute-start | bytes 7208 | tf_op jit(solution)/shard_map/ppermute | solution.py:17
  363.4 45.1 %collective-permute-start.21 = (f32[3,20,1,128]{3,2,1,0:T(1,128)}, f32[3,20,1,128]{3,2,1,0:T(1,128)}, u32[]{:S(2)}, u32[]{:S(2)}) collective-permute-start(f32[3,20,1,128]{3,2,1,0:T(1,128)} %get-tuple-element.140), channel_id=1, source_target_pairs={{8,0},{16,8},{24,16},{9,1},{17,9},{25,17},{10,2},{18,10},{26,18},{... | collective-permute-start | bytes 92168 | tf_op jit(solution)/shard_map/ppermute | solution.py:18
  364.7 43.8 %collective-permute-start.20 = (f32[3,20,1,128]{3,2,1,0:T(1,128)}, f32[3,20,1,128]{3,2,1,0:T(1,128)}, u32[]{:S(2)}, u32[]{:S(2)}) collective-permute-start(f32[3,20,1,128]{3,2,1,0:T(1,128)} %get-tuple-element.139), channel_id=1, source_target_pairs={{0,8},{8,16},{16,24},{1,9},{9,17},{17,25},{2,10},{10,18},{18,26},{... | collective-permute-start | bytes 92168 | tf_op jit(solution)/shard_map/ppermute | solution.py:17
  412.1 24.7 %collective-permute-start.22 = (f32[3,20,10,1]{3,2,1,0:T(8,128)}, f32[3,20,10,1]{3,2,1,0:T(8,128)}, u32[]{:S(2)}, u32[]{:S(2)}) collective-permute-start(f32[3,20,10,1]{3,2,1,0:T(8,128)} %get-tuple-element.94), channel_id=1, source_target_pairs={{0,1},{1,2},{2,3},{3,4},{4,5},{5,6},{6,7},{8,9},{9,10},{10,11},{11... | collective-permute-start | bytes 7208 | tf_op jit(solution)/shard_map/ppermute | solution.py:17
  442.0 34.1 %collective-permute-start.25 = (f32[3,20,1,128]{3,2,1,0:T(1,128)}, f32[3,20,1,128]{3,2,1,0:T(1,128)}, u32[]{:S(2)}, u32[]{:S(2)}) collective-permute-start(f32[3,20,1,128]{3,2,1,0:T(1,128)} %get-tuple-element.134), channel_id=1, source_target_pairs={{8,0},{16,8},{24,16},{9,1},{17,9},{25,17},{10,2},{18,10},{26,18},{... | collective-permute-start | bytes 92168 | tf_op jit(solution)/shard_map/ppermute | solution.py:18
  443.3 32.8 %collective-permute-start.24 = (f32[3,20,1,128]{3,2,1,0:T(1,128)}, f32[3,20,1,128]{3,2,1,0:T(1,128)}, u32[]{:S(2)}, u32[]{:S(2)}) collective-permute-start(f32[3,20,1,128]{3,2,1,0:T(1,128)} %get-tuple-element.133), channel_id=1, source_target_pairs={{0,8},{8,16},{16,24},{1,9},{9,17},{17,25},{2,10},{10,18},{18,26},{... | collective-permute-start | bytes 92168 | tf_op jit(solution)/shard_map/ppermute | solution.py:17
  479.6 24.7 %collective-permute-start.26 = (f32[3,20,10,1]{3,2,1,0:T(8,128)}, f32[3,20,10,1]{3,2,1,0:T(8,128)}, u32[]{:S(2)}, u32[]{:S(2)}) collective-permute-start(f32[3,20,10,1]{3,2,1,0:T(8,128)} %get-tuple-element.92), channel_id=1, source_target_pairs={{0,1},{1,2},{2,3},{3,4},{4,5},{5,6},{6,7},{8,9},{9,10},{10,11},{11... | collective-permute-start | bytes 7208 | tf_op jit(solution)/shard_map/ppermute | solution.py:17
  509.5 33.8 %collective-permute-start.29 = (f32[3,20,1,128]{3,2,1,0:T(1,128)}, f32[3,20,1,128]{3,2,1,0:T(1,128)}, u32[]{:S(2)}, u32[]{:S(2)}) collective-permute-start(f32[3,20,1,128]{3,2,1,0:T(1,128)} %get-tuple-element.128), channel_id=1, source_target_pairs={{8,0},{16,8},{24,16},{9,1},{17,9},{25,17},{10,2},{18,10},{26,18},{... | collective-permute-start | bytes 92168 | tf_op jit(solution)/shard_map/ppermute | solution.py:18
  510.8 32.5 %collective-permute-start.28 = (f32[3,20,1,128]{3,2,1,0:T(1,128)}, f32[3,20,1,128]{3,2,1,0:T(1,128)}, u32[]{:S(2)}, u32[]{:S(2)}) collective-permute-start(f32[3,20,1,128]{3,2,1,0:T(1,128)} %get-tuple-element.127), channel_id=1, source_target_pairs={{0,8},{8,16},{16,24},{1,9},{9,17},{17,25},{2,10},{10,18},{18,26},{... | collective-permute-start | bytes 92168 | tf_op jit(solution)/shard_map/ppermute | solution.py:17
  546.8 24.7 %collective-permute-start.30 = (f32[3,20,10,1]{3,2,1,0:T(8,128)}, f32[3,20,10,1]{3,2,1,0:T(8,128)}, u32[]{:S(2)}, u32[]{:S(2)}) collective-permute-start(f32[3,20,10,1]{3,2,1,0:T(8,128)} %get-tuple-element.90), channel_id=1, source_target_pairs={{0,1},{1,2},{2,3},{3,4},{4,5},{5,6},{6,7},{8,9},{9,10},{10,11},{11... | collective-permute-start | bytes 7208 | tf_op jit(solution)/shard_map/ppermute | solution.py:17
  602.1 23.2 %collective-permute-start.34 = (f32[3,20,10,1]{3,2,1,0:T(8,128)S(1)}, f32[3,20,10,1]{3,2,1,0:T(8,128)S(1)}, u32[]{:S(2)}, u32[]{:S(2)}) collective-permute-start(f32[3,20,10,1]{3,2,1,0:T(8,128)S(1)} %get-tuple-element.88), channel_id=1, source_target_pairs={{0,1},{1,2},{2,3},{3,4},{4,5},{5,6},{6,7},{8,9},{9,10},{10,11},{11... | collective-permute-start | bytes 7208 | tf_op jit(solution)/shard_map/ppermute | solution.py:17
  (211 other events, 2296.1 us)
where the time goes:
time: 685 us; the launch traced here: 673 us
  starting transfers between devices  183 us (27%)
  waiting for transfers between devices  168 us (25%)
  other arithmetic  126 us (18%)
  local copies, waits for them, and re-layouts  106 us (15%)
  blocking collectives  78.8 us (12%)
  between operations  11.6 us (2%)
    ppermute x18, waiting for transfers between devices, extended(): before = lax.ppermute(last, axis, up)  84.6 us
    psum x2, blocking collectives, on_device(): numer, denom = lax.psum((local_numer, local_denom), ('gx', 'gy'))  78.8 us
    ppermute x18, starting transfers between devices, extended(): before = lax.ppermute(last, axis, up)  78.2 us
    all_to_all x9, starting transfers between devices, to_owners(): lax.all_to_all(buffer, ('gx', 'gy'), split_axis=1, concat_axis=1, tiled=T...  51.1 us
    ppermute x18, waiting for transfers between devices, extended(): after = lax.ppermute(leading, axis, down)  46.4 us
    all_to_all x9, waiting for transfers between devices, to_owners(): lax.all_to_all(buffer, ('gx', 'gy'), split_axis=1, concat_axis=1, tiled=T...  34.1 us
    all_to_all x8, starting transfers between devices, on_device(): lax.all_to_all(seg_new[perf_seg[0]], ('gx', 'gy'), split_axis=1, concat_a...  29.2 us
    ppermute x18, starting transfers between devices, extended(): after = lax.ppermute(leading, axis, down)  24.3 us
  transfers between devices with their start and end apart: 53, of which 27 were waited for; matrix products, arithmetic and copies ran while one was open for 25% of the time, Pallas kernels for 0%

commit v1 on v0

v1 whole, which is shorter than its diff:
```python
import functools

import jax
import jax.numpy as jnp
from jax import lax
from jax.experimental import pallas as pl
from jax.experimental.pallas import tpu as pltpu
from jax.sharding import PartitionSpec as P

SWEEPS = 4
SUB, LANE = 8, 128
SLOTS = 8
MESH = pl.DeviceIdType.MESH
F32 = jnp.float32


def apply3(mat, vec):
    return [mat[3 * r] * vec[0] + mat[3 * r + 1] * vec[1] + mat[3 * r + 2] * vec[2] for r in range(3)]


def inverse3(m):
    a, b, c, d, e, f, g, h, i = m
    first = e * i - f * h
    second = f * g - d * i
    third = d * h - e * g
    inv = 1.0 / (a * first + b * second + c * third)
    entries = [
        first, c * h - b * i, b * f - c * e,
        second, a * i - c * g, c * d - a * f,
        third, b * g - a * h, a * e - b * d,
    ]
    return [entry * inv for entry in entries]


def kernel(
    nx, ny, layers, seg_rows,
    rhs, diag, mob, trans, cell_s, cell_v, perf_pi, perf_seg, parent, seg_trans, seg_rhs,
    out_u, out_w,
    v, tx, ty, tz, part, res, v4, a4, dinv, dd, mm, tt, ty_edge, into,
    onehot, feed, pi_row, k_of, idx, rows, send, recv, ypack, yrecv, xrecv,
    turn_i, turn_f, seg, sums,
    halo_send, halo_recv, msg_send, msg_recv,
):
    n = nx * ny
    my_x, my_y = lax.axis_index("gx"), lax.axis_index("gy")
    me = my_x * ny + my_y
    barrier = pltpu.get_barrier_semaphore()

    def partner(j):
        pos = lax.rem(me + j, n)
        return (lax.div(pos, ny), lax.rem(pos, ny))

    def greet(j, carry):
        pl.semaphore_signal(barrier, inc=1, device_id=partner(j), device_id_type=MESH)
        return carry

    xrecv[...] = jnp.zeros_like(xrecv)
    yrecv[...] = jnp.zeros_like(yrecv)
    lax.fori_loop(1, n, greet, 0)

    has_x = [my_x > 0, my_x < nx - 1]
    has_y = [my_y > 0, my_y < ny - 1]

    def halos(slot):
        below_x, above_x = lax.max(my_x - 1, 0), lax.min(my_x + 1, nx - 1)
        below_y, above_y = lax.max(my_y - 1, 0), lax.min(my_y + 1, ny - 1)

        def copy(src, dst, way, device):
            return pltpu.make_async_remote_copy(
                src_ref=src, dst_ref=dst, send_sem=halo_send.at[slot, way],
                recv_sem=halo_recv.at[slot, way], device_id=device, device_id_type=MESH,
            )

        return [
            (has_x[1], has_x[0], copy(
                tx.at[:, :, SUB - 1:SUB, :], xrecv.at[slot, :, :, 0:1, :], 0, (above_x, my_y))),
            (has_x[0], has_x[1], copy(
                tx.at[:, :, 0:1, :], xrecv.at[slot, :, :, SUB - 1:SUB, :], 1, (below_x, my_y))),
            (has_y[1], has_y[0], copy(ypack.at[slot], yrecv.at[slot, 0], 2, (my_x, above_y))),
            (has_y[0], has_y[1], copy(ypack.at[slot], yrecv.at[slot, 1], 3, (my_x, below_y))),
        ]

    def send_halos(slot):
        for to, _, copy in halos(slot):
            pl.when(to)(copy.start)

    def wait_halos(slot):
        for to, come, copy in halos(slot):
            pl.when(come)(copy.wait_recv)
            pl.when(to)(copy.wait_send)

    def send_rows(slot):
        def one(j, carry):
            target = partner(j)
            pos = target[0] * ny + target[1]
            pltpu.make_async_remote_copy(
                src_ref=send.at[slot, pl.ds(pos, 1), :], dst_ref=recv.at[slot, pl.ds(me, 1), :],
                send_sem=msg_send.at[slot], recv_sem=msg_recv.at[slot],
                device_id=target, device_id_type=MESH,
            ).start()
            return carry

        lax.fori_loop(1, n, one, 0)

    def wait_rows(slot):
        some = pl.ds(0, n - 1)
        copy = pltpu.make_async_remote_copy(
            src_ref=send.at[slot, some, :], dst_ref=recv.at[slot, some, :],
            send_sem=msg_send.at[slot], recv_sem=msg_recv.at[slot],
            device_id=(my_x, my_y), device_id_type=MESH,
        )
        copy.wait_recv()
        copy.wait_send()

    row_n = lax.broadcasted_iota(jnp.int32, (n, LANE), 0)
    lane_n = lax.broadcasted_iota(jnp.int32, (n, LANE), 1)

    def arrived(slot):
        return jnp.where(row_n == me, send[slot], recv[slot])

    turn_i[...] = jnp.zeros_like(turn_i)
    turn_f[...] = jnp.zeros_like(turn_f)
    turn_i[0:SLOTS, 0:n] = cell_v[0]
    turn_i[SLOTS:2 * SLOTS, 0:n] = perf_seg[0]
    turn_f[0:SLOTS, 0:n] = perf_pi[0]
    places = turn_i[...].T[0:n, :]
    weights = turn_f[...].T[0:n, :]
    send[0] = weights
    pl.semaphore_wait(barrier, n - 1)
    send_rows(0)

    lanes_at = lax.rem(places, LANE)
    idx[...] = lanes_at
    spread = jnp.zeros((n, LANE), F32)
    slot_of = jnp.zeros((n, LANE), jnp.int32)
    for k in range(SLOTS):
        here = lane_n == lanes_at[:, k:k + 1]
        spread = spread + jnp.where(here, weights[:, k:k + 1], 0.0)
        slot_of = jnp.where(here, SLOTS + k, slot_of)
    pi_row[...] = spread
    k_of[...] = slot_of
    row_id = lax.div(cell_v[0][0:1, :], LANE)
    grid_rows = lax.broadcasted_iota(jnp.int32, (layers * SUB, n), 0)
    onehot[...] = jnp.where(grid_rows == row_id, 1.0, 0.0).astype(jnp.bfloat16)

    def scatter(field):
        table = onehot[...]
        high = field.astype(jnp.bfloat16)
        rest = field - high.astype(F32)
        mid = rest.astype(jnp.bfloat16)
        low = (rest - mid.astype(F32)).astype(jnp.bfloat16)
        total = jnp.dot(table, low, preferred_element_type=F32)
        total = total + jnp.dot(table, mid, preferred_element_type=F32)
        return total + jnp.dot(table, high, preferred_element_type=F32)

    into[...] = scatter(spread).reshape(layers, SUB, LANE)

    zc = 4 if layers % 4 == 0 else 1
    chunks = [slice(z, z + zc) for z in range(0, layers, zc)]
    lane = lax.broadcasted_iota(jnp.int32, (SUB, LANE), 1)
    row = lax.broadcasted_iota(jnp.int32, (SUB, LANE), 0)
    edge = (lane == 0) | (lane == LANE - 1)

    tz[:, 0] = jnp.zeros((3, SUB, LANE), F32)
    tz[:, layers + 1] = jnp.zeros((3, SUB, LANE), F32)

    def flat(zs):
        return slice(zs.start * SUB, zs.stop * SUB)

    def publish(zs, vec, packed):
        mv = apply3([mm[i, zs] for i in range(9)], vec)
        for c in range(3):
            v[c, flat(zs), :] = vec[c].reshape(zc * SUB, LANE)
            tx[c, zs] = tt[0, zs] * mv[c]
            along = tt[1, zs] * mv[c]
            ty[c, zs] = along
            tz[c, zs.start + 1:zs.stop + 1] = tt[2, zs] * mv[c]
            for z in range(zs.start, zs.stop):
                shift = (2 * (c * layers + z)) % LANE
                moved = along[z - zs.start]
                if shift:
                    moved = pltpu.roll(moved, shift, 1)
                mine = (lane == (shift - 1) % LANE) | (lane == shift)
                packed = jnp.where(mine, moved, packed)
        return packed

    packed = jnp.zeros((SUB, LANE), F32)
    for zs in chunks:
        dense = [diag[i, zs].astype(F32) for i in range(9)]
        mobile = [mob[i, zs].astype(F32) for i in range(9)]
        inv = inverse3(dense)
        perf = into[zs]
        for i in range(9):
            dinv[i, zs] = inv[i]
            mm[i, zs] = mobile[i]
            dd[i, zs] = dense[i] + mobile[i] * perf if i % 3 == 0 else dense[i]
        for i in range(3):
            tt[i, zs] = trans[i, zs].astype(F32)
        ty_edge[zs] = jnp.where(edge, tt[1, zs], 0.0)
        packed = publish(zs, apply3(inv, [rhs[c, zs] for c in range(3)]), packed)
    ypack[1] = packed

    seg[...] = jnp.zeros_like(seg)
    seg[0, 0:seg_rows, :] = jnp.where(parent[...] >= 0, seg_trans[...], 0.0)
    seg[2, 0:seg_rows, :] = seg_trans[...]
    seg[3, 0:seg_rows, :] = seg_rhs[...]

    def before(x):
        moved = pltpu.roll(x, 1, 1)
        return jnp.where(lane == 0, pltpu.roll(moved, 1, 0), moved)

    def after(x):
        moved = pltpu.roll(x, LANE - 1, 1)
        return jnp.where(lane == LANE - 1, pltpu.roll(moved, SUB - 1, 0), moved)

    def tile(parts):
        total = jnp.zeros((SUB, LANE), F32)
        for r in range(seg_rows):
            total = jnp.where(row == r, jnp.sum(parts[r], axis=0, keepdims=True), total)
        return total

    seg[1] = after(seg[0])
    wait_rows(0)
    came = arrived(0)
    parts = [jnp.zeros((n, LANE), F32) for _ in range(seg_rows)]
    for k in range(SLOTS):
        goes = places[:, SLOTS + k:SLOTS + k + 1]
        for r in range(seg_rows):
            term = jnp.where(lane_n + r * LANE == goes, came[:, k:k + 1], 0.0)
            feed[k, r] = term
            parts[r] = parts[r] + term
    turn_i[0:n, :] = lax.div(places, LANE)
    seg[2] = jnp.where(row < seg_rows, seg[2] + seg[1] + tile(parts), 1.0)
    seg[4] = seg[3] / seg[2]
    sums[...] = jnp.zeros_like(sums)

    def fill(slot):
        for o in range(n):
            at = lax.div(cell_s[0, 0, o], LANE)
            rows[o:o + 1, :] = v[0, pl.ds(at, 1), :]
        where_to = idx[...]
        which = turn_i[0:n, :]
        state = seg[4]
        row_vals = jnp.take_along_axis(rows[...], where_to, axis=1, mode="promise_in_bounds")
        seg_vals = jnp.zeros((n, LANE), F32)
        for r in range(seg_rows):
            whole = jnp.broadcast_to(state[r:r + 1, :], (n, LANE))
            got = jnp.take_along_axis(whole, where_to, axis=1, mode="promise_in_bounds")
            seg_vals = jnp.where(which == r, got, seg_vals)
        total = jnp.broadcast_to(sums[0:1, :], (n, LANE))
        send[slot] = jnp.where(
            lane_n < SLOTS, row_vals, jnp.where(lane_n < 2 * SLOTS, seg_vals, total))

    fill(1)

    def inside():
        for zs in chunks:
            vec = [v[c, flat(zs), :].reshape(zc, SUB, LANE) for c in range(3)]
            pulled = apply3([dd[i, zs] for i in range(9)], vec)
            for c in range(3):
                x, y = tx[c, zs], ty[c, zs]
                near_x = (
                    jnp.where(row == 0, 0.0, pltpu.roll(x, 1, 1))
                    + jnp.where(row == SUB - 1, 0.0, pltpu.roll(x, SUB - 1, 1)))
                near_y = (
                    jnp.where(lane == 0, 0.0, pltpu.roll(y, 1, 2))
                    + jnp.where(lane == LANE - 1, 0.0, pltpu.roll(y, LANE - 1, 2)))
                near_z = tz[c, zs] + tz[c, zs.start + 2:zs.stop + 2]
                part[c, zs] = (
                    rhs[c, zs] - pulled[c]
                    + (tt[0, zs] * near_x + tt[1, zs] * near_y + tt[2, zs] * near_z))

    def segments(came):
        parts = [jnp.zeros((n, LANE), F32) for _ in range(seg_rows)]
        for k in range(SLOTS):
            value = jnp.broadcast_to(came[:, k:k + 1], (n, LANE))
            for r in range(seg_rows):
                parts[r] = parts[r] + value * feed[k, r]
        g = seg[4]
        return (
            seg[3] - seg[2] * g + seg[0] * before(g) + seg[1] * after(g) + tile(parts))

    def receive(slot):
        wait_rows(slot)
        came = arrived(slot)
        pressure = jnp.take_along_axis(came, k_of[...], axis=1, mode="promise_in_bounds")
        into[...] = scatter(pi_row[...] * pressure).reshape(layers, SUB, LANE)
        seg[5] = segments(came)
        wait_halos(slot)
        border = jnp.where(
            lax.rem(lane, 2) == 0,
            pltpu.roll(yrecv[slot, 0], 1, 1), pltpu.roll(yrecv[slot, 1], LANE - 1, 1))
        return came, border

    def residual(zs, slot, border):
        vec = []
        for c in range(3):
            total = part[c, zs] + tt[0, zs] * xrecv[slot, c, zs] + mm[3 * c, zs] * into[zs]
            sides = []
            for z in range(zs.start, zs.stop):
                shift = (2 * (c * layers + z)) % LANE
                sides.append(pltpu.roll(border, LANE - shift, 1) if shift else border)
            total = total + ty_edge[zs] * jnp.stack(sides)
            res[c, zs] = total
            vec.append(total)
        return vec

    def put_sums(numer, denom):
        first = jnp.sum(jnp.sum(numer, axis=0, keepdims=True), axis=1, keepdims=True)
        second = jnp.sum(jnp.sum(denom, axis=0, keepdims=True), axis=1, keepdims=True)
        sums[...] = jnp.where(
            lane == 2 * SLOTS, first, jnp.where(lane == 2 * SLOTS + 1, second, 0.0))

    def ratio(came):
        total = jnp.sum(came, axis=0, keepdims=True)
        return total[:, 2 * SLOTS:2 * SLOTS + 1] / total[:, 2 * SLOTS + 1:2 * SLOTS + 2]

    def keep_state():
        for c in range(3):
            for zs in chunks:
                v4[c, zs] = v[c, flat(zs), :].reshape(zc, SUB, LANE)
        seg[6] = seg[4]

    def keep_residual():
        numer = seg[3] * (seg[3] - seg[5])
        denom = (seg[3] - seg[5]) * (seg[3] - seg[5])
        seg[7] = seg[5]
        for c in range(3):
            for zs in chunks:
                last, start = res[c, zs], rhs[c, zs]
                a4[c, zs] = last
                diff = start - last
                numer = numer + jnp.sum(start * diff, axis=0)
                denom = denom + jnp.sum(diff * diff, axis=0)
        put_sums(numer, denom)

    def exchange(k, slot):
        send_rows(slot)
        send_halos(slot)
        inside()
        pl.when(k == SWEEPS)(keep_state)
        pl.when(k == SWEEPS + 1)(keep_residual)

    def sweep(k, carry):
        slot = lax.rem(k, 2)
        exchange(k, slot)
        came, border = receive(slot)

        @pl.when(k == SWEEPS + 2)
        def _():
            sums[1:2, :] = jnp.broadcast_to(ratio(came), (1, LANE))

        seg[4] = seg[4] + seg[5] / seg[2]
        packed = jnp.zeros((SUB, LANE), F32)
        for zs in chunks:
            step = apply3([dinv[i, zs] for i in range(9)], residual(zs, slot, border))
            vec = [v[c, flat(zs), :].reshape(zc, SUB, LANE) + step[c] for c in range(3)]
            packed = publish(zs, vec, packed)
        ypack[1 - slot] = packed
        fill(1 - slot)
        return carry

    last = 2 * SWEEPS
    lax.fori_loop(1, last, sweep, 0)
    slot = last % 2
    omega = sums[1:2, :]
    exchange(last, slot)
    _, border = receive(slot)

    def mix(old, new):
        return old + omega * (new - old)

    start, middle, end = seg[3], seg[7], seg[5]
    first = mix(start, middle)
    diff = first - mix(middle, end)
    numer, denom = first * diff, diff * diff
    for zs in chunks:
        now = residual(zs, slot, border)
        for c in range(3):
            middle = a4[c, zs]
            first = mix(rhs[c, zs], middle)
            diff = first - mix(middle, now[c])
            numer = numer + jnp.sum(first * diff, axis=0)
            denom = denom + jnp.sum(diff * diff, axis=0)
    put_sums(numer, denom)
    send[1] = jnp.broadcast_to(sums[0:1, :], (n, LANE))
    send_rows(1)
    wait_rows(1)
    second = jnp.broadcast_to(ratio(arrived(1)), (1, LANE))

    def combine(middle, end):
        base = omega * middle
        return base + second * (mix(middle, end) - base)

    for c in range(3):
        for zs in chunks:
            out_u[c, zs] = combine(v4[c, zs], v[c, flat(zs), :].reshape(zc, SUB, LANE))
    out_w[...] = combine(seg[6], seg[4])[0:seg_rows, :]


def on_device(
    rhs, diag_block, mobility, trans, perf_cell, perf_pi, perf_seg, seg_parent, seg_trans, seg_rhs
):
    nx, ny = lax.axis_size("gx"), lax.axis_size("gy")
    n = nx * ny
    layers = rhs.shape[1]
    seg_rows = seg_rhs.shape[0] // LANE
    tiles = (seg_rows, LANE)
    cells = (layers, SUB, LANE)
    vmem = pl.BlockSpec(memory_space=pltpu.VMEM)
    scratch = lambda *shape: pltpu.VMEM(shape, F32)
    u, w = pl.pallas_call(
        functools.partial(kernel, nx, ny, layers, seg_rows),
        out_shape=[
            jax.ShapeDtypeStruct(rhs.shape, F32), jax.ShapeDtypeStruct(tiles, F32)],
        in_specs=[vmem] * 4 + [pl.BlockSpec(memory_space=pltpu.SMEM)] + [vmem] * 6,
        out_specs=[vmem] * 2,
        scratch_shapes=[
            scratch(3, layers * SUB, LANE), scratch(3, *cells), scratch(3, *cells),
            scratch(3, layers + 2, SUB, LANE), scratch(3, *cells), scratch(3, *cells),
            scratch(3, *cells), scratch(3, *cells), scratch(9, *cells), scratch(9, *cells),
            scratch(9, *cells), scratch(3, *cells), scratch(*cells), scratch(*cells),
            pltpu.VMEM((layers * SUB, n), jnp.bfloat16),
            scratch(SLOTS, seg_rows, n, LANE), scratch(n, LANE),
            pltpu.VMEM((n, LANE), jnp.int32), pltpu.VMEM((n, LANE), jnp.int32),
            scratch(n, LANE), scratch(2, n, LANE), scratch(2, n, LANE),
            scratch(2, SUB, LANE), scratch(2, 2, SUB, LANE), scratch(2, 3, *cells),
            pltpu.VMEM((LANE, LANE), jnp.int32), scratch(LANE, LANE),
            scratch(8, SUB, LANE), scratch(SUB, LANE),
            pltpu.SemaphoreType.DMA((2, 4)), pltpu.SemaphoreType.DMA((2, 4)),
            pltpu.SemaphoreType.DMA((2,)), pltpu.SemaphoreType.DMA((2,)),
        ],
        compiler_params=pltpu.CompilerParams(
            collective_id=0, has_side_effects=True, vmem_limit_bytes=40 * 1024 * 1024),
        name="sweeps",
    )(
        rhs, diag_block, mobility, trans, perf_cell, perf_cell, perf_pi, perf_seg,
        seg_parent.reshape(tiles), seg_trans.reshape(tiles), seg_rhs.reshape(tiles),
    )
    return u, w.reshape(-1)


def solution(mesh):
    return jax.shard_map(
        on_device,
        mesh=mesh,
        in_specs=(
            P(None, None, "gx", "gy"),
            P(None, None, "gx", "gy"),
            P(None, None, "gx", "gy"),
            P(None, None, "gx", "gy"),
            P(("gx", "gy"), None, None),
            P(("gx", "gy"), None, None),
            P(("gx", "gy"), None, None),
            P(("gx", "gy")),
            P(("gx", "gy")),
            P(("gx", "gy")),
        ),
        out_specs=(P(None, None, "gx", "gy"), P(("gx", "gy"))),
        check_vma=False,
    )
```

time: 685 us -> 68.3 us (0.10); the launches traced: 673 us -> 67.9 us
  starting transfers between devices: 183 us -> 0 us
  waiting for transfers between devices: 168 us -> 0 us
  other arithmetic: 126 us -> 0 us
  local copies, waits for them, and re-layouts: 106 us -> 8.49 us
  blocking collectives: 78.8 us -> 0 us
  Pallas kernels: 0 us -> 58.7 us
  between operations: 11.6 us -> 0.67 us
    ppermute x36 -> x0, waiting for transfers between devices: 131 us -> none  [the longest x18 84.6 us: extended(): before = lax.ppermute(last, axis, up)]
    ppermute x36 -> x0, starting transfers between devices: 103 us -> none  [the longest x18 78.2 us: extended(): before = lax.ppermute(last, axis, up)]
    all_to_all x17 -> x0, starting transfers between devices: 80.3 us -> none  [the longest x9 51.1 us: to_owners(): lax.all_to_all(buffer, ('gx', 'gy'), split_axis=1, concat_axis=1, tiled=T...]
    psum x2 -> x0, blocking collectives: 78.8 us -> none  [on_device(): numer, denom = lax.psum((local_numer, local_denom), ('gx', 'gy'))]
    scatter-add x26 -> x0, other arithmetic: 64.6 us -> none  [the longest x8 21.7 us: on_device(): into_cells = jnp.zeros((cells_count,), jnp.float32).at[cell_index].add(fl...]
    pallas_call x0 -> x1, Pallas kernels: none -> 58.7 us  [on_device(): pl.pallas_call(functools.partial(kernel, nx, ny, layers, seg_rows), out_s...]
    gather x32 -> x0, local copies, waits for them, and re-layouts: 56.8 us -> none  [the longest x16 20.9 us: on_device(): advance_field[0].reshape(-1)[cell_index] - advance_slot_state.reshape(-1)]
    all_to_all x17 -> x0, waiting for transfers between devices: 36.7 us -> none  [the longest x9 34.1 us: to_owners(): lax.all_to_all(buffer, ('gx', 'gy'), split_axis=1, concat_axis=1, tiled=T...]
  transfers between devices with their start and end apart: 53 -> 0, of which waited for: 27 -> 0; matrix products, arithmetic and copies ran while one was open for 25% -> 0% of each run, Pallas kernels for 0% -> 0%
where the time goes in v1:
time: 68.3 us; the launch traced here: 67.9 us
  Pallas kernels  58.7 us (86%)
  local copies, waits for them, and re-layouts  8.49 us (12%)
    pallas_call x1, Pallas kernels, on_device(): pl.pallas_call(functools.partial(kernel, nx, ny, layers, seg_rows), out_s...  58.7 us
    unnamed x22, local copies, waits for them, and re-layouts  8.49 us

profile of v1, /device:TPU:0, one launch (start us, length us, event | category | flops | bytes accessed | tf_op | source)
XLA Modules:
  0.0 67.9 jit_solution(12335034448529809746)
XLA Ops:
  0.6 0.0 copy-start.4
  0.6 0.0 copy-start.7
  0.7 0.7 copy-done.4
  1.3 0.0 copy-done.7
  1.3 0.0 copy-start
  1.3 1.0 %copy-done = bf16[9,20,8,128]{3,2,1,0:T(8,128)(2,1)S(1)} copy-done((bf16[9,20,8,128]{3,2,1,0:T(8,128)(2,1)S(1)}, bf16[9,20,8,128]{3,2,1,0:T(8,128)(2,1)}, u32[]{:S(2)}) %copy-start) | copy-done | bytes 368664
  2.3 0.0 copy-start.1
  2.3 1.0 %copy-done.1 = bf16[9,20,8,128]{3,2,1,0:T(8,128)(2,1)S(1)} copy-done((bf16[9,20,8,128]{3,2,1,0:T(8,128)(2,1)S(1)}, bf16[9,20,8,128]{3,2,1,0:T(8,128)(2,1)}, u32[]{:S(2)}) %copy-start.1) | copy-done | bytes 368664
  3.3 0.0 copy-start.2
  3.3 0.9 %copy-done.2 = f32[3,20,8,128]{3,2,1,0:T(8,128)S(1)} copy-done((f32[3,20,8,128]{3,2,1,0:T(8,128)S(1)}, f32[3,20,8,128]{3,2,1,0:T(8,128)}, u32[]{:S(2)}) %copy-start.2) | copy-done | bytes 245784
  4.2 0.0 copy-start.3
  4.3 0.9 %copy-done.3 = bf16[3,20,8,128]{3,2,1,0:T(8,128)(2,1)S(1)} copy-done((bf16[3,20,8,128]{3,2,1,0:T(8,128)(2,1)S(1)}, bf16[3,20,8,128]{3,2,1,0:T(8,128)(2,1)}, u32[]{:S(2)}) %copy-start.3) | copy-done | bytes 122904
  5.2 0.0 copy-start.5
  5.2 0.7 %copy-done.5 = f32[1,8,32]{2,1,0:T(8,128)S(1)} copy-done((f32[1,8,32]{2,1,0:T(8,128)S(1)}, f32[1,8,32]{2,1,0:T(8,128)}, u32[]{:S(2)}) %copy-start.5) | copy-done | bytes 1048
  5.8 0.0 copy-start.6
  5.8 0.7 %copy-done.6 = s32[1,8,32]{2,1,0:T(8,128)S(1)} copy-done((s32[1,8,32]{2,1,0:T(8,128)S(1)}, s32[1,8,32]{2,1,0:T(8,128)}, u32[]{:S(2)}) %copy-start.6) | copy-done | bytes 1048
  6.5 0.0 copy-start.8
  6.5 0.7 copy-done.8
  7.2 0.0 copy-start.9
  7.2 0.7 copy-done.9
  7.9 58.7 %sweeps.1 = (f32[3,20,8,128]{3,2,1,0:T(8,128)S(1)}, f32[2,128]{1,0:T(2,128)S(1)}) custom-call(f32[3,20,8,128]{3,2,1,0:T(8,128)S(1)} %copy-done.2, bf16[9,20,8,128]{3,2,1,0:T(8,128)(2,1)S(1)} %copy-done, bf16[9,20,8,128]{3,2,1,0:T(8,128)(2,1)S(1)} %copy-done.1, bf16[3,20,8,128]{3,2,1,0:T(8,128)(2,1)S(1)} %copy-done.3, s32[1,8,32]{2,1,0:T(8,128)S(1)} %copy-done.4, ...), custom_call_target="tpu_custom_call" | custom-call | tf_op jit(solution)/shard_map/sweeps/pallas_call | solution.py:412
  66.6 0.7 %copy.14 = f32[3,20,8,128]{3,2,1,0:T(8,128)} copy(f32[3,20,8,128]{3,2,1,0:T(8,128)S(1)} %get-tuple-element.8) | data formatting | bytes 491520
  67.3 0.6 copy.15
Async XLA Ops:
  0.6 0.7 %copy-start.4 = (s32[1,8,32]{2,1,0:T(8,128)S(1)}, s32[1,8,32]{2,1,0:T(8,128)}, u32[]{:S(2)}) copy-start(s32[1,8,32]{2,1,0:T(8,128)} %cell_v.1) | copy-start | bytes 3076
  0.6 0.7 %copy-start.7 = (s32[256]{0:T(256)S(1)}, s32[256]{0:T(256)}, u32[]{:S(2)}) copy-start(s32[256]{0:T(256)} %param.17) | copy-start | bytes 3076
  1.3 1.0 %copy-start = (bf16[9,20,8,128]{3,2,1,0:T(8,128)(2,1)S(1)}, bf16[9,20,8,128]{3,2,1,0:T(8,128)(2,1)}, u32[]{:S(2)}) copy-start(bf16[9,20,8,128]{3,2,1,0:T(8,128)(2,1)} %diag.1) | copy-start | bytes 1105924
  2.3 1.0 %copy-start.1 = (bf16[9,20,8,128]{3,2,1,0:T(8,128)(2,1)S(1)}, bf16[9,20,8,128]{3,2,1,0:T(8,128)(2,1)}, u32[]{:S(2)}) copy-start(bf16[9,20,8,128]{3,2,1,0:T(8,128)(2,1)} %mob.1) | copy-start | bytes 1105924
  3.3 0.9 %copy-start.2 = (f32[3,20,8,128]{3,2,1,0:T(8,128)S(1)}, f32[3,20,8,128]{3,2,1,0:T(8,128)}, u32[]{:S(2)}) copy-start(f32[3,20,8,128]{3,2,1,0:T(8,128)} %rhs.1) | copy-start | bytes 737284
  4.2 0.9 %copy-start.3 = (bf16[3,20,8,128]{3,2,1,0:T(8,128)(2,1)S(1)}, bf16[3,20,8,128]{3,2,1,0:T(8,128)(2,1)}, u32[]{:S(2)}) copy-start(bf16[3,20,8,128]{3,2,1,0:T(8,128)(2,1)} %trans.1) | copy-start | bytes 368644
  5.2 0.7 %copy-start.5 = (f32[1,8,32]{2,1,0:T(8,128)S(1)}, f32[1,8,32]{2,1,0:T(8,128)}, u32[]{:S(2)}) copy-start(f32[1,8,32]{2,1,0:T(8,128)} %perf_pi.1) | copy-start | bytes 3076
  5.8 0.7 %copy-start.6 = (s32[1,8,32]{2,1,0:T(8,128)S(1)}, s32[1,8,32]{2,1,0:T(8,128)}, u32[]{:S(2)}) copy-start(s32[1,8,32]{2,1,0:T(8,128)} %perf_seg.1) | copy-start | bytes 3076
  6.5 0.7 copy-start.8
  7.2 0.7 copy-start.9

commit v2 on v1

--- a/solution.py
+++ b/solution.py
@@ -34,29 +34,38 @@
 
 def kernel(
     nx, ny, layers, seg_rows,
+    rhs_h, diag_h, mob_h, trans_h, cell_h, pi_h, seg_h, parent_h, seg_trans_h, seg_rhs_h,
+    out_u, out_w,
     rhs, diag, mob, trans, cell_s, cell_v, perf_pi, perf_seg, parent, seg_trans, seg_rhs,
-    out_u, out_w,
-    v, tx, ty, tz, part, res, v4, a4, dinv, dd, mm, tt, ty_edge, into,
-    onehot, feed, pi_row, k_of, idx, rows, send, recv, ypack, yrecv, xrecv,
+    v, tx, ty, tz, part, res, v4, a4, dinv, dd, mm, kk, tt, ty_edge, into,
+    onehot, same, feed, pi_row, k_of, idx, rows, k_rows, flow, send, recv, ypack, yrecv, xrecv,
     turn_i, turn_f, seg, sums,
-    halo_send, halo_recv, msg_send, msg_recv,
+    halo_send, halo_recv, msg_send, msg_recv, load_sem,
 ):
     n = nx * ny
     my_x, my_y = lax.axis_index("gx"), lax.axis_index("gy")
     me = my_x * ny + my_y
     barrier = pltpu.get_barrier_semaphore()
 
-    def partner(j):
-        pos = lax.rem(me + j, n)
-        return (lax.div(pos, ny), lax.rem(pos, ny))
-
-    def greet(j, carry):
-        pl.semaphore_signal(barrier, inc=1, device_id=partner(j), device_id_type=MESH)
-        return carry
+    loads = [
+        pltpu.make_async_copy(src, dst, load_sem.at[i])
+        for i, (src, dst) in enumerate([
+            (cell_h, cell_v), (pi_h, perf_pi), (seg_h, perf_seg), (cell_h, cell_s),
+            (diag_h, diag), (mob_h, mob), (trans_h, trans), (rhs_h, rhs),
+            (parent_h, parent), (seg_trans_h, seg_trans), (seg_rhs_h, seg_rhs),
+        ])
+    ]
+    for load in loads:
+        load.start()
+
+    at_x = [my_x] + [lax.rem(my_x + a, nx) for a in range(1, nx)]
+    at_y = [my_y] + [lax.rem(my_y + b, ny) for b in range(1, ny)]
+    partners = [(at_x[a], at_y[b]) for b in range(ny) for a in range(nx) if a + b]
 
     xrecv[...] = jnp.zeros_like(xrecv)
     yrecv[...] = jnp.zeros_like(yrecv)
-    lax.fori_loop(1, n, greet, 0)
+    for target in partners:
+        pl.semaphore_signal(barrier, inc=1, device_id=target, device_id_type=MESH)
 
     has_x = [my_x > 0, my_x < nx - 1]
     has_y = [my_y > 0, my_y < ny - 1]
@@ -90,17 +99,13 @@
             pl.when(to)(copy.wait_send)
 
     def send_rows(slot):
-        def one(j, carry):
-            target = partner(j)
+        for target in partners:
             pos = target[0] * ny + target[1]
             pltpu.make_async_remote_copy(
                 src_ref=send.at[slot, pl.ds(pos, 1), :], dst_ref=recv.at[slot, pl.ds(me, 1), :],
                 send_sem=msg_send.at[slot], recv_sem=msg_recv.at[slot],
                 device_id=target, device_id_type=MESH,
             ).start()
-            return carry
-
-        lax.fori_loop(1, n, one, 0)
 
     def wait_rows(slot):
         some = pl.ds(0, n - 1)
@@ -120,6 +125,8 @@
 
     turn_i[...] = jnp.zeros_like(turn_i)
     turn_f[...] = jnp.zeros_like(turn_f)
+    for load in loads[:4]:
+        load.wait()
     turn_i[0:SLOTS, 0:n] = cell_v[0]
     turn_i[SLOTS:2 * SLOTS, 0:n] = perf_seg[0]
     turn_f[0:SLOTS, 0:n] = perf_pi[0]
@@ -140,20 +147,24 @@
     pi_row[...] = spread
     k_of[...] = slot_of
     row_id = lax.div(cell_v[0][0:1, :], LANE)
-    grid_rows = lax.broadcasted_iota(jnp.int32, (layers * SUB, n), 0)
+    row_id = jnp.concatenate([row_id] * 3, axis=1)
+    grid_rows = lax.broadcasted_iota(jnp.int32, (layers * SUB, 3 * n), 0)
     onehot[...] = jnp.where(grid_rows == row_id, 1.0, 0.0).astype(jnp.bfloat16)
-
-    def scatter(field):
-        table = onehot[...]
+    same[...] = jnp.where(lax.div(places[:, 0:1], LANE) == row_id, 1.0, 0.0).astype(jnp.bfloat16)
+
+    def split(field):
         high = field.astype(jnp.bfloat16)
         rest = field - high.astype(F32)
         mid = rest.astype(jnp.bfloat16)
         low = (rest - mid.astype(F32)).astype(jnp.bfloat16)
-        total = jnp.dot(table, low, preferred_element_type=F32)
-        total = total + jnp.dot(table, mid, preferred_element_type=F32)
-        return total + jnp.dot(table, high, preferred_element_type=F32)
-
-    into[...] = scatter(spread).reshape(layers, SUB, LANE)
+        return jnp.concatenate([high, mid, low], axis=0)
+
+    def scatter():
+        total = jnp.dot(onehot[...], flow[...], preferred_element_type=F32)
+        into[...] = total.reshape(layers, SUB, LANE)
+
+    flow[...] = split(spread)
+    scatter()
 
     zc = 4 if layers % 4 == 0 else 1
     chunks = [slice(z, z + zc) for z in range(0, layers, zc)]
@@ -184,7 +195,8 @@
                 packed = jnp.where(mine, moved, packed)
         return packed
 
-    packed = jnp.zeros((SUB, LANE), F32)
+    for load in loads[4:]:
+        load.wait()
     for zs in chunks:
         dense = [diag[i, zs].astype(F32) for i in range(9)]
         mobile = [mob[i, zs].astype(F32) for i in range(9)]
@@ -197,8 +209,20 @@
         for i in range(3):
             tt[i, zs] = trans[i, zs].astype(F32)
         ty_edge[zs] = jnp.where(edge, tt[1, zs], 0.0)
-        packed = publish(zs, apply3(inv, [rhs[c, zs] for c in range(3)]), packed)
-    ypack[1] = packed
+        gain = apply3(inv, [mobile[0], mobile[3], mobile[6]])
+        vec = apply3(inv, [rhs[c, zs] for c in range(3)])
+        for c in range(3):
+            kk[c, flat(zs), :] = gain[c].reshape(zc * SUB, LANE)
+            v[c, flat(zs), :] = vec[c].reshape(zc * SUB, LANE)
+    flow[...] = jnp.zeros_like(flow)
+
+    def pick_rows(source, target):
+        for o in range(n):
+            at = lax.div(cell_s[0, 0, o], LANE)
+            target[o:o + 1, :] = source[0, pl.ds(at, 1), :]
+
+    pick_rows(kk, k_rows)
+    pick_rows(v, rows)
 
     seg[...] = jnp.zeros_like(seg)
     seg[0, 0:seg_rows, :] = jnp.where(parent[...] >= 0, seg_trans[...], 0.0)
@@ -235,13 +259,12 @@
     sums[...] = jnp.zeros_like(sums)
 
     def fill(slot):
-        for o in range(n):
-            at = lax.div(cell_s[0, 0, o], LANE)
-            rows[o:o + 1, :] = v[0, pl.ds(at, 1), :]
         where_to = idx[...]
         which = turn_i[0:n, :]
         state = seg[4]
-        row_vals = jnp.take_along_axis(rows[...], where_to, axis=1, mode="promise_in_bounds")
+        there = rows[...] + k_rows[...] * jnp.dot(
+            same[...], flow[...], preferred_element_type=F32)
+        row_vals = jnp.take_along_axis(there, where_to, axis=1, mode="promise_in_bounds")
         seg_vals = jnp.zeros((n, LANE), F32)
         for r in range(seg_rows):
             whole = jnp.broadcast_to(state[r:r + 1, :], (n, LANE))
@@ -252,6 +275,18 @@
             lane_n < SLOTS, row_vals, jnp.where(lane_n < 2 * SLOTS, seg_vals, total))
 
     fill(1)
+
+    def advance(slot):
+        scatter()
+        packed = jnp.zeros((SUB, LANE), F32)
+        for zs in chunks:
+            vec = [
+                v[c, flat(zs), :].reshape(zc, SUB, LANE)
+                + kk[c, flat(zs), :].reshape(zc, SUB, LANE) * into[zs]
+                for c in range(3)
+            ]
+            packed = publish(zs, vec, packed)
+        ypack[slot] = packed
 
     def inside():
         for zs in chunks:
@@ -284,26 +319,30 @@
         wait_rows(slot)
         came = arrived(slot)
         pressure = jnp.take_along_axis(came, k_of[...], axis=1, mode="promise_in_bounds")
-        into[...] = scatter(pi_row[...] * pressure).reshape(layers, SUB, LANE)
+        flow[...] = split(pi_row[...] * pressure)
         seg[5] = segments(came)
+        return came
+
+    def borders(slot, last):
         wait_halos(slot)
         border = jnp.where(
             lax.rem(lane, 2) == 0,
             pltpu.roll(yrecv[slot, 0], 1, 1), pltpu.roll(yrecv[slot, 1], LANE - 1, 1))
-        return came, border
-
-    def residual(zs, slot, border):
-        vec = []
-        for c in range(3):
-            total = part[c, zs] + tt[0, zs] * xrecv[slot, c, zs] + mm[3 * c, zs] * into[zs]
-            sides = []
-            for z in range(zs.start, zs.stop):
-                shift = (2 * (c * layers + z)) % LANE
-                sides.append(pltpu.roll(border, LANE - shift, 1) if shift else border)
-            total = total + ty_edge[zs] * jnp.stack(sides)
-            res[c, zs] = total
-            vec.append(total)
-        return vec
+        for zs in chunks:
+            vec = []
+            for c in range(3):
+                total = part[c, zs] + tt[0, zs] * xrecv[slot, c, zs]
+                sides = []
+                for z in range(zs.start, zs.stop):
+                    shift = (2 * (c * layers + z)) % LANE
+                    sides.append(pltpu.roll(border, LANE - shift, 1) if shift else border)
+                total = total + ty_edge[zs] * jnp.stack(sides)
+                res[c, zs] = total
+                vec.append(total)
+            if not last:
+                step = apply3([dinv[i, zs] for i in range(9)], vec)
+                for c in range(3):
+                    v[c, flat(zs), :] = v[c, flat(zs), :] + step[c].reshape(zc * SUB, LANE)
 
     def put_sums(numer, denom):
         first = jnp.sum(jnp.sum(numer, axis=0, keepdims=True), axis=1, keepdims=True)
@@ -327,36 +366,33 @@
         seg[7] = seg[5]
         for c in range(3):
             for zs in chunks:
-                last, start = res[c, zs], rhs[c, zs]
+                last, start = res[c, zs] + mm[3 * c, zs] * into[zs], rhs[c, zs]
                 a4[c, zs] = last
                 diff = start - last
                 numer = numer + jnp.sum(start * diff, axis=0)
                 denom = denom + jnp.sum(diff * diff, axis=0)
         put_sums(numer, denom)
 
-    def exchange(k, slot):
+    def exchange(k, slot, last):
         send_rows(slot)
+        advance(slot)
         send_halos(slot)
-        inside()
         pl.when(k == SWEEPS)(keep_state)
         pl.when(k == SWEEPS + 1)(keep_residual)
+        inside()
+        borders(slot, last)
 
     def sweep(k, carry):
         slot = lax.rem(k, 2)
-        exchange(k, slot)
-        came, border = receive(slot)
+        exchange(k, slot, False)
+        pick_rows(v, rows)
+        came = receive(slot)
 
         @pl.when(k == SWEEPS + 2)
         def _():
             sums[1:2, :] = jnp.broadcast_to(ratio(came), (1, LANE))
 
         seg[4] = seg[4] + seg[5] / seg[2]
-        packed = jnp.zeros((SUB, LANE), F32)
-        for zs in chunks:
-            step = apply3([dinv[i, zs] for i in range(9)], residual(zs, slot, border))
-            vec = [v[c, flat(zs), :].reshape(zc, SUB, LANE) + step[c] for c in range(3)]
-            packed = publish(zs, vec, packed)
-        ypack[1 - slot] = packed
         fill(1 - slot)
         return carry
 
@@ -364,8 +400,9 @@
     lax.fori_loop(1, last, sweep, 0)
     slot = last % 2
     omega = sums[1:2, :]
-    exchange(last, slot)
-    _, border = receive(slot)
+    exchange(last, slot, True)
+    receive(slot)
+    scatter()
 
     def mix(old, new):
         return old + omega * (new - old)
@@ -375,11 +412,10 @@
     diff = first - mix(middle, end)
     numer, denom = first * diff, diff * diff
     for zs in chunks:
-        now = residual(zs, slot, border)
         for c in range(3):
             middle = a4[c, zs]
             first = mix(rhs[c, zs], middle)
-            diff = first - mix(middle, now[c])
+            diff = first - mix(middle, res[c, zs] + mm[3 * c, zs] * into[zs])
             numer = numer + jnp.sum(first * diff, axis=0)
             denom = denom + jnp.sum(diff * diff, axis=0)
     put_sums(numer, denom)
@@ -408,33 +444,46 @@
     tiles = (seg_rows, LANE)
     cells = (layers, SUB, LANE)
     vmem = pl.BlockSpec(memory_space=pltpu.VMEM)
-    scratch = lambda *shape: pltpu.VMEM(shape, F32)
+    far = pl.BlockSpec(memory_space=pltpu.HBM)
+
+    def scratch(*shape, kind=F32):
+        return pltpu.VMEM(shape, kind)
+
+    slots = perf_cell.shape
+    half, whole = jnp.bfloat16, jnp.int32
     u, w = pl.pallas_call(
         functools.partial(kernel, nx, ny, layers, seg_rows),
         out_shape=[
             jax.ShapeDtypeStruct(rhs.shape, F32), jax.ShapeDtypeStruct(tiles, F32)],
-        in_specs=[vmem] * 4 + [pl.BlockSpec(memory_space=pltpu.SMEM)] + [vmem] * 6,
+        in_specs=[far] * 10,
         out_specs=[vmem] * 2,
         scratch_shapes=[
+            scratch(3, *cells), scratch(9, *cells, kind=half), scratch(9, *cells, kind=half),
+            scratch(3, *cells, kind=half), pltpu.SMEM(slots, whole),
+            scratch(*slots, kind=whole), scratch(*slots), scratch(*slots, kind=whole),
+            scratch(*tiles, kind=whole), scratch(*tiles), scratch(*tiles),
             scratch(3, layers * SUB, LANE), scratch(3, *cells), scratch(3, *cells),
             scratch(3, layers + 2, SUB, LANE), scratch(3, *cells), scratch(3, *cells),
             scratch(3, *cells), scratch(3, *cells), scratch(9, *cells), scratch(9, *cells),
-            scratch(9, *cells), scratch(3, *cells), scratch(*cells), scratch(*cells),
-            pltpu.VMEM((layers * SUB, n), jnp.bfloat16),
+            scratch(9, *cells), scratch(3, layers * SUB, LANE), scratch(3, *cells),
+            scratch(*cells), scratch(*cells),
+            scratch(layers * SUB, 3 * n, kind=half), scratch(n, 3 * n, kind=half),
             scratch(SLOTS, seg_rows, n, LANE), scratch(n, LANE),
-            pltpu.VMEM((n, LANE), jnp.int32), pltpu.VMEM((n, LANE), jnp.int32),
-            scratch(n, LANE), scratch(2, n, LANE), scratch(2, n, LANE),
+            scratch(n, LANE, kind=whole), scratch(n, LANE, kind=whole),
+            scratch(n, LANE), scratch(n, LANE), scratch(3 * n, LANE, kind=half),
+            scratch(2, n, LANE), scratch(2, n, LANE),
             scratch(2, SUB, LANE), scratch(2, 2, SUB, LANE), scratch(2, 3, *cells),
-            pltpu.VMEM((LANE, LANE), jnp.int32), scratch(LANE, LANE),
+            scratch(LANE, LANE, kind=whole), scratch(LANE, LANE),
             scratch(8, SUB, LANE), scratch(SUB, LANE),
             pltpu.SemaphoreType.DMA((2, 4)), pltpu.SemaphoreType.DMA((2, 4)),
             pltpu.SemaphoreType.DMA((2,)), pltpu.SemaphoreType.DMA((2,)),
+            pltpu.SemaphoreType.DMA((11,)),
         ],
         compiler_params=pltpu.CompilerParams(
             collective_id=0, has_side_effects=True, vmem_limit_bytes=40 * 1024 * 1024),
         name="sweeps",
     )(
-        rhs, diag_block, mobility, trans, perf_cell, perf_cell, perf_pi, perf_seg,
+        rhs, diag_block, mobility, trans, perf_cell, perf_pi, perf_seg,
         seg_parent.reshape(tiles), seg_trans.reshape(tiles), seg_rhs.reshape(tiles),
     )
     return u, w.reshape(-1)

time: 68.3 us -> 65.2 us (0.955)
  Pallas kernels: 58.7 us -> 55.7 us
    pallas_call x1, Pallas kernels: 58.7 us -> 55.7 us  [on_device(): pl.pallas_call(functools.partial(kernel, nx, ny, layers, seg_rows), out_s...]
where the time goes in v2:
time: 65.2 us; the launch traced here: 64.8 us
  Pallas kernels  55.7 us (85%)
  local copies, waits for them, and re-layouts  8.49 us (13%)
  between operations  0.67 us (1%)
    pallas_call x1, Pallas kernels, on_device(): pl.pallas_call(functools.partial(kernel, nx, ny, layers, seg_rows), out_s...  55.7 us
    unnamed x22, local copies, waits for them, and re-layouts  8.49 us

profile of v2, /device:TPU:0, one launch (start us, length us, event | category | flops | bytes accessed | tf_op | source)
XLA Modules:
  0.0 64.8 jit_solution(6035763183326277330)
XLA Ops:
  0.6 0.0 copy-start.4
  0.6 0.0 copy-start.7
  0.7 0.7 %copy-done.4 = s32[1,8,32]{2,1,0:T(8,128)S(1)} copy-done((s32[1,8,32]{2,1,0:T(8,128)S(1)}, s32[1,8,32]{2,1,0:T(8,128)}, u32[]{:S(2)}) %copy-start.4) | copy-done | bytes 1048
  1.3 0.0 copy-done.7
  1.3 0.0 copy-start
  1.3 1.0 %copy-done = bf16[9,20,8,128]{3,2,1,0:T(8,128)(2,1)S(1)} copy-done((bf16[9,20,8,128]{3,2,1,0:T(8,128)(2,1)S(1)}, bf16[9,20,8,128]{3,2,1,0:T(8,128)(2,1)}, u32[]{:S(2)}) %copy-start) | copy-done | bytes 368664
  2.3 0.0 copy-start.1
  2.3 1.0 %copy-done.1 = bf16[9,20,8,128]{3,2,1,0:T(8,128)(2,1)S(1)} copy-done((bf16[9,20,8,128]{3,2,1,0:T(8,128)(2,1)S(1)}, bf16[9,20,8,128]{3,2,1,0:T(8,128)(2,1)}, u32[]{:S(2)}) %copy-start.1) | copy-done | bytes 368664
  3.3 0.0 copy-start.2
  3.3 0.9 %copy-done.2 = f32[3,20,8,128]{3,2,1,0:T(8,128)S(1)} copy-done((f32[3,20,8,128]{3,2,1,0:T(8,128)S(1)}, f32[3,20,8,128]{3,2,1,0:T(8,128)}, u32[]{:S(2)}) %copy-start.2) | copy-done | bytes 245784
  4.2 0.0 copy-start.3
  4.3 0.9 %copy-done.3 = bf16[3,20,8,128]{3,2,1,0:T(8,128)(2,1)S(1)} copy-done((bf16[3,20,8,128]{3,2,1,0:T(8,128)(2,1)S(1)}, bf16[3,20,8,128]{3,2,1,0:T(8,128)(2,1)}, u32[]{:S(2)}) %copy-start.3) | copy-done | bytes 122904
  5.2 0.0 copy-start.5
  5.2 0.7 %copy-done.5 = f32[1,8,32]{2,1,0:T(8,128)S(1)} copy-done((f32[1,8,32]{2,1,0:T(8,128)S(1)}, f32[1,8,32]{2,1,0:T(8,128)}, u32[]{:S(2)}) %copy-start.5) | copy-done | bytes 1048
  5.8 0.0 copy-start.6
  5.8 0.7 %copy-done.6 = s32[1,8,32]{2,1,0:T(8,128)S(1)} copy-done((s32[1,8,32]{2,1,0:T(8,128)S(1)}, s32[1,8,32]{2,1,0:T(8,128)}, u32[]{:S(2)}) %copy-start.6) | copy-done | bytes 1048
  6.5 0.0 copy-start.8
  6.5 0.7 %copy-done.8 = f32[256]{0:T(256)S(1)} copy-done((f32[256]{0:T(256)S(1)}, f32[256]{0:T(256)}, u32[]{:S(2)}) %copy-start.8) | copy-done | bytes 1048
  7.2 0.0 copy-start.9
  7.2 0.7 %copy-done.9 = f32[256]{0:T(256)S(1)} copy-done((f32[256]{0:T(256)S(1)}, f32[256]{0:T(256)}, u32[]{:S(2)}) %copy-start.9) | copy-done | bytes 1048
  7.9 55.7 %sweeps.1 = (f32[3,20,8,128]{3,2,1,0:T(8,128)S(1)}, f32[2,128]{1,0:T(2,128)S(1)}) custom-call(f32[3,20,8,128]{3,2,1,0:T(8,128)S(1)} %copy-done.2, bf16[9,20,8,128]{3,2,1,0:T(8,128)(2,1)S(1)} %copy-done, bf16[9,20,8,128]{3,2,1,0:T(8,128)(2,1)S(1)} %copy-done.1, bf16[3,20,8,128]{3,2,1,0:T(8,128)(2,1)S(1)} %copy-done.3, s32[1,8,32]{2,1,0:T(8,128)S(1)} %copy-done.4, ...), custom_call_target="tpu_custom_call" | custom-call | tf_op jit(solution)/shard_map/sweeps/pallas_call | solution.py:454
  63.5 0.7 %copy.14 = f32[3,20,8,128]{3,2,1,0:T(8,128)} copy(f32[3,20,8,128]{3,2,1,0:T(8,128)S(1)} %get-tuple-element.8) | data formatting | bytes 491520
  64.2 0.6 copy.15
Async XLA Ops:
  0.6 0.7 %copy-start.4 = (s32[1,8,32]{2,1,0:T(8,128)S(1)}, s32[1,8,32]{2,1,0:T(8,128)}, u32[]{:S(2)}) copy-start(s32[1,8,32]{2,1,0:T(8,128)} %cell_h.1) | copy-start | bytes 3076
  0.6 0.7 %copy-start.7 = (s32[256]{0:T(256)S(1)}, s32[256]{0:T(256)}, u32[]{:S(2)}) copy-start(s32[256]{0:T(256)} %param.17) | copy-start | bytes 3076
  1.3 1.0 %copy-start = (bf16[9,20,8,128]{3,2,1,0:T(8,128)(2,1)S(1)}, bf16[9,20,8,128]{3,2,1,0:T(8,128)(2,1)}, u32[]{:S(2)}) copy-start(bf16[9,20,8,128]{3,2,1,0:T(8,128)(2,1)} %diag_h.1) | copy-start | bytes 1105924
  2.3 1.0 %copy-start.1 = (bf16[9,20,8,128]{3,2,1,0:T(8,128)(2,1)S(1)}, bf16[9,20,8,128]{3,2,1,0:T(8,128)(2,1)}, u32[]{:S(2)}) copy-start(bf16[9,20,8,128]{3,2,1,0:T(8,128)(2,1)} %mob_h.1) | copy-start | bytes 1105924
  3.3 0.9 %copy-start.2 = (f32[3,20,8,128]{3,2,1,0:T(8,128)S(1)}, f32[3,20,8,128]{3,2,1,0:T(8,128)}, u32[]{:S(2)}) copy-start(f32[3,20,8,128]{3,2,1,0:T(8,128)} %rhs_h.1) | copy-start | bytes 737284
  4.2 0.9 %copy-start.3 = (bf16[3,20,8,128]{3,2,1,0:T(8,128)(2,1)S(1)}, bf16[3,20,8,128]{3,2,1,0:T(8,128)(2,1)}, u32[]{:S(2)}) copy-start(bf16[3,20,8,128]{3,2,1,0:T(8,128)(2,1)} %trans_h.1) | copy-start | bytes 368644
  5.2 0.7 %copy-start.5 = (f32[1,8,32]{2,1,0:T(8,128)S(1)}, f32[1,8,32]{2,1,0:T(8,128)}, u32[]{:S(2)}) copy-start(f32[1,8,32]{2,1,0:T(8,128)} %pi_h.1) | copy-start | bytes 3076
  5.8 0.7 %copy-start.6 = (s32[1,8,32]{2,1,0:T(8,128)S(1)}, s32[1,8,32]{2,1,0:T(8,128)}, u32[]{:S(2)}) copy-start(s32[1,8,32]{2,1,0:T(8,128)} %seg_h.1) | copy-start | bytes 3076
  6.5 0.7 %copy-start.8 = (f32[256]{0:T(256)S(1)}, f32[256]{0:T(256)}, u32[]{:S(2)}) copy-start(f32[256]{0:T(256)} %param.18) | copy-start | bytes 3076
  7.2 0.7 %copy-start.9 = (f32[256]{0:T(256)S(1)}, f32[256]{0:T(256)}, u32[]{:S(2)}) copy-start(f32[256]{0:T(256)} %param.19) | copy-start | bytes 3076

commit v3 on v2

--- a/solution.py
+++ b/solution.py
@@ -38,7 +38,7 @@
     out_u, out_w,
     rhs, diag, mob, trans, cell_s, cell_v, perf_pi, perf_seg, parent, seg_trans, seg_rhs,
     v, tx, ty, tz, part, res, v4, a4, dinv, dd, mm, kk, tt, ty_edge, into,
-    onehot, same, feed, pi_row, k_of, idx, rows, k_rows, flow, send, recv, ypack, yrecv, xrecv,
+    onehot, same, feed, pi_row, k_of, idx, rows, k_rows, flow, send, hop, recv, ypack, yrecv, xrecv,
     turn_i, turn_f, seg, sums,
     halo_send, halo_recv, msg_send, msg_recv, load_sem,
 ):
@@ -60,7 +60,7 @@
 
     at_x = [my_x] + [lax.rem(my_x + a, nx) for a in range(1, nx)]
     at_y = [my_y] + [lax.rem(my_y + b, ny) for b in range(1, ny)]
-    partners = [(at_x[a], at_y[b]) for b in range(ny) for a in range(nx) if a + b]
+    partners = [(x, my_y) for x in at_x[1:]] + [(my_x, y) for y in at_y[1:]]
 
     xrecv[...] = jnp.zeros_like(xrecv)
     yrecv[...] = jnp.zeros_like(yrecv)
@@ -98,30 +98,42 @@
             pl.when(come)(copy.wait_recv)
             pl.when(to)(copy.wait_send)
 
+    def step_copy(slot, step, src, dst, device):
+        return pltpu.make_async_remote_copy(
+            src_ref=src, dst_ref=dst, send_sem=msg_send.at[slot, step],
+            recv_sem=msg_recv.at[slot, step], device_id=device, device_id_type=MESH,
+        )
+
+    def put_rows(slot, values):
+        send[slot] = values.reshape(nx, ny, LANE)
+        hop[slot, my_x] = send[slot, my_x]
+
     def send_rows(slot):
-        for target in partners:
-            pos = target[0] * ny + target[1]
-            pltpu.make_async_remote_copy(
-                src_ref=send.at[slot, pl.ds(pos, 1), :], dst_ref=recv.at[slot, pl.ds(me, 1), :],
-                send_sem=msg_send.at[slot], recv_sem=msg_recv.at[slot],
-                device_id=target, device_id_type=MESH,
-            ).start()
-
-    def wait_rows(slot):
-        some = pl.ds(0, n - 1)
-        copy = pltpu.make_async_remote_copy(
-            src_ref=send.at[slot, some, :], dst_ref=recv.at[slot, some, :],
-            send_sem=msg_send.at[slot], recv_sem=msg_recv.at[slot],
-            device_id=(my_x, my_y), device_id_type=MESH,
-        )
+        for x in at_x[1:]:
+            step_copy(slot, 0, send.at[slot, x], hop.at[slot, my_x], (x, my_y)).start()
+
+    def pass_rows(slot):
+        some = pl.ds(0, nx - 1)
+        copy = step_copy(slot, 0, send.at[slot, some], hop.at[slot, some], (my_x, my_y))
         copy.wait_recv()
         copy.wait_send()
-
-    row_n = lax.broadcasted_iota(jnp.int32, (n, LANE), 0)
+        for y in at_y[1:]:
+            step_copy(
+                slot, 1, hop.at[slot, :, pl.ds(y, 1), :], recv.at[slot, :, pl.ds(my_y, 1), :],
+                (my_x, y)).start()
+
+    def wait_rows(slot):
+        some = pl.ds(0, ny - 1)
+        copy = step_copy(
+            slot, 1, hop.at[slot, :, some, :], recv.at[slot, :, some, :], (my_x, my_y))
+        copy.wait_recv()
+        copy.wait_send()
+
     lane_n = lax.broadcasted_iota(jnp.int32, (n, LANE), 1)
 
     def arrived(slot):
-        return jnp.where(row_n == me, send[slot], recv[slot])
+        from_y = lax.broadcasted_iota(jnp.int32, (nx, ny, LANE), 1)
+        return jnp.where(from_y == my_y, hop[slot], recv[slot]).reshape(n, LANE)
 
     turn_i[...] = jnp.zeros_like(turn_i)
     turn_f[...] = jnp.zeros_like(turn_f)
@@ -132,8 +144,8 @@
     turn_f[0:SLOTS, 0:n] = perf_pi[0]
     places = turn_i[...].T[0:n, :]
     weights = turn_f[...].T[0:n, :]
-    send[0] = weights
-    pl.semaphore_wait(barrier, n - 1)
+    put_rows(0, weights)
+    pl.semaphore_wait(barrier, nx + ny - 2)
     send_rows(0)
 
     lanes_at = lax.rem(places, LANE)
@@ -165,6 +177,7 @@
 
     flow[...] = split(spread)
     scatter()
+    pass_rows(0)
 
     zc = 4 if layers % 4 == 0 else 1
     chunks = [slice(z, z + zc) for z in range(0, layers, zc)]
@@ -271,8 +284,8 @@
             got = jnp.take_along_axis(whole, where_to, axis=1, mode="promise_in_bounds")
             seg_vals = jnp.where(which == r, got, seg_vals)
         total = jnp.broadcast_to(sums[0:1, :], (n, LANE))
-        send[slot] = jnp.where(
-            lane_n < SLOTS, row_vals, jnp.where(lane_n < 2 * SLOTS, seg_vals, total))
+        put_rows(slot, jnp.where(
+            lane_n < SLOTS, row_vals, jnp.where(lane_n < 2 * SLOTS, seg_vals, total)))
 
     fill(1)
 
@@ -288,7 +301,7 @@
             packed = publish(zs, vec, packed)
         ypack[slot] = packed
 
-    def inside():
+    def inside(chunks):
         for zs in chunks:
             vec = [v[c, flat(zs), :].reshape(zc, SUB, LANE) for c in range(3)]
             pulled = apply3([dd[i, zs] for i in range(9)], vec)
@@ -379,7 +392,9 @@
         send_halos(slot)
         pl.when(k == SWEEPS)(keep_state)
         pl.when(k == SWEEPS + 1)(keep_residual)
-        inside()
+        inside(chunks[:2])
+        pass_rows(slot)
+        inside(chunks[2:])
         borders(slot, last)
 
     def sweep(k, carry):
@@ -419,8 +434,9 @@
             numer = numer + jnp.sum(first * diff, axis=0)
             denom = denom + jnp.sum(diff * diff, axis=0)
     put_sums(numer, denom)
-    send[1] = jnp.broadcast_to(sums[0:1, :], (n, LANE))
+    put_rows(1, jnp.broadcast_to(sums[0:1, :], (n, LANE)))
     send_rows(1)
+    pass_rows(1)
     wait_rows(1)
     second = jnp.broadcast_to(ratio(arrived(1)), (1, LANE))
 
@@ -471,16 +487,16 @@
             scratch(SLOTS, seg_rows, n, LANE), scratch(n, LANE),
             scratch(n, LANE, kind=whole), scratch(n, LANE, kind=whole),
             scratch(n, LANE), scratch(n, LANE), scratch(3 * n, LANE, kind=half),
-            scratch(2, n, LANE), scratch(2, n, LANE),
+            scratch(2, nx, ny, LANE), scratch(2, nx, ny, LANE), scratch(2, nx, ny, LANE),
             scratch(2, SUB, LANE), scratch(2, 2, SUB, LANE), scratch(2, 3, *cells),
             scratch(LANE, LANE, kind=whole), scratch(LANE, LANE),
             scratch(8, SUB, LANE), scratch(SUB, LANE),
             pltpu.SemaphoreType.DMA((2, 4)), pltpu.SemaphoreType.DMA((2, 4)),
-            pltpu.SemaphoreType.DMA((2,)), pltpu.SemaphoreType.DMA((2,)),
+            pltpu.SemaphoreType.DMA((2, 2)), pltpu.SemaphoreType.DMA((2, 2)),
             pltpu.SemaphoreType.DMA((11,)),
         ],
         compiler_params=pltpu.CompilerParams(
-            collective_id=0, has_side_effects=True, vmem_limit_bytes=40 * 1024 * 1024),
+            collective_id=0, has_side_effects=True, vmem_limit_bytes=62 * 1024 * 1024),
         name="sweeps",
     )(
         rhs, diag_block, mobility, trans, perf_cell, perf_pi, perf_seg,

time: 65.2 us -> 79.4 us (1.22)
  Pallas kernels: 55.7 us -> 76.3 us
  local copies, waits for them, and re-layouts: 8.49 us -> 2.22 us
    pallas_call x1, Pallas kernels: 55.7 us -> 76.3 us  [on_device(): pl.pallas_call(functools.partial(kernel, nx, ny, layers, seg_rows), out_s...]
    unnamed x22 -> x4, local copies, waits for them, and re-layouts: 8.49 us -> 2.22 us
where the time goes in v3:
time: 79.4 us; the launch traced here: 79.2 us
  Pallas kernels  76.3 us (96%)
  local copies, waits for them, and re-layouts  2.22 us (3%)
    pallas_call x1, Pallas kernels, on_device(): pl.pallas_call(functools.partial(kernel, nx, ny, layers, seg_rows), out_s...  76.3 us
    unnamed x4, local copies, waits for them, and re-layouts  2.22 us

profile of v3, /device:TPU:0, one launch (start us, length us, event | category | flops | bytes accessed | tf_op | source)
XLA Modules:
  0.0 79.2 jit_solution(1053598915414980820)
XLA Ops:
  0.6 76.3 %sweeps.1 = (f32[3,20,8,128]{3,2,1,0:T(8,128)}, f32[2,128]{1,0:T(2,128)}) custom-call(f32[3,20,8,128]{3,2,1,0:T(8,128)} %rhs_h.1, bf16[9,20,8,128]{3,2,1,0:T(8,128)(2,1)} %diag_h.1, bf16[9,20,8,128]{3,2,1,0:T(8,128)(2,1)} %mob_h.1, bf16[3,20,8,128]{3,2,1,0:T(8,128)(2,1)} %trans_h.1, s32[1,8,32]{2,1,0:T(8,128)} %cell_h.1, f32[1,8,32]{2,1,0:T(8,128)} %pi_h.1, ...), custom_call_target="tpu_custom_call" | custom-call | tf_op jit(solution)/shard_map/sweeps/pallas_call | solution.py:470
  76.9 0.0 copy-start
  77.0 1.7 %copy.14 = f32[3,20,8,128]{3,2,1,0:T(8,128)} copy(f32[3,20,8,128]{3,2,1,0:T(8,128)} %get-tuple-element.8) | data formatting | bytes 491520
  78.6 0.0 copy-done
  78.6 0.6 copy.15
Async XLA Ops:
  76.9 1.7 %copy-start = (f32[2,128]{1,0:T(2,128)S(1)}, f32[2,128]{1,0:T(2,128)}, u32[]{:S(2)}) copy-start(f32[2,128]{1,0:T(2,128)} %get-tuple-element.5) | copy-start | bytes 3076

commit v4 on v2

--- a/solution.py
+++ b/solution.py
@@ -60,7 +60,8 @@
 
     at_x = [my_x] + [lax.rem(my_x + a, nx) for a in range(1, nx)]
     at_y = [my_y] + [lax.rem(my_y + b, ny) for b in range(1, ny)]
-    partners = [(at_x[a], at_y[b]) for b in range(ny) for a in range(nx) if a + b]
+    far_first = sorted(range(ny), key=lambda b: -min(b, ny - b))
+    partners = [(at_x[a], at_y[b]) for b in far_first for a in reversed(range(nx)) if a + b]
 
     xrecv[...] = jnp.zeros_like(xrecv)
     yrecv[...] = jnp.zeros_like(yrecv)
@@ -274,8 +275,6 @@
         send[slot] = jnp.where(
             lane_n < SLOTS, row_vals, jnp.where(lane_n < 2 * SLOTS, seg_vals, total))
 
-    fill(1)
-
     def advance(slot):
         scatter()
         packed = jnp.zeros((SUB, LANE), F32)
@@ -305,22 +304,25 @@
                     rhs[c, zs] - pulled[c]
                     + (tt[0, zs] * near_x + tt[1, zs] * near_y + tt[2, zs] * near_z))
 
-    def segments(came):
+    def rest():
+        g = seg[4]
+        return seg[3] - seg[2] * g + seg[0] * before(g) + seg[1] * after(g)
+
+    def fed(came):
         parts = [jnp.zeros((n, LANE), F32) for _ in range(seg_rows)]
         for k in range(SLOTS):
             value = jnp.broadcast_to(came[:, k:k + 1], (n, LANE))
             for r in range(seg_rows):
                 parts[r] = parts[r] + value * feed[k, r]
-        g = seg[4]
-        return (
-            seg[3] - seg[2] * g + seg[0] * before(g) + seg[1] * after(g) + tile(parts))
+        return tile(parts)
 
     def receive(slot):
+        base = rest()
         wait_rows(slot)
         came = arrived(slot)
         pressure = jnp.take_along_axis(came, k_of[...], axis=1, mode="promise_in_bounds")
         flow[...] = split(pi_row[...] * pressure)
-        seg[5] = segments(came)
+        seg[5] = base + fed(came)
         return came
 
     def borders(slot, last):
@@ -374,9 +376,10 @@
         put_sums(numer, denom)
 
     def exchange(k, slot, last):
-        send_rows(slot)
+        fill(slot)
         advance(slot)
         send_halos(slot)
+        send_rows(slot)
         pl.when(k == SWEEPS)(keep_state)
         pl.when(k == SWEEPS + 1)(keep_residual)
         inside()
@@ -393,7 +396,6 @@
             sums[1:2, :] = jnp.broadcast_to(ratio(came), (1, LANE))
 
         seg[4] = seg[4] + seg[5] / seg[2]
-        fill(1 - slot)
         return carry
 
     last = 2 * SWEEPS
@@ -480,7 +482,7 @@
             pltpu.SemaphoreType.DMA((11,)),
         ],
         compiler_params=pltpu.CompilerParams(
-            collective_id=0, has_side_effects=True, vmem_limit_bytes=40 * 1024 * 1024),
+            collective_id=0, has_side_effects=True, vmem_limit_bytes=62 * 1024 * 1024),
         name="sweeps",
     )(
         rhs, diag_block, mobility, trans, perf_cell, perf_pi, perf_seg,

time: 65.2 us -> 60.7 us (0.931)
  local copies, waits for them, and re-layouts: 8.49 us -> 2.22 us
  Pallas kernels: 55.7 us -> 57.6 us
    unnamed x22 -> x4, local copies, waits for them, and re-layouts: 8.49 us -> 2.22 us
    pallas_call x1, Pallas kernels: 55.7 us -> 57.6 us  [on_device(): pl.pallas_call(functools.partial(kernel, nx, ny, layers, seg_rows), out_s...]
where the time goes in v4:
time: 60.7 us; the launch traced here: 60.5 us
  Pallas kernels  57.6 us (95%)
  local copies, waits for them, and re-layouts  2.22 us (4%)
  between operations  0.65 us (1%)
    pallas_call x1, Pallas kernels, on_device(): pl.pallas_call(functools.partial(kernel, nx, ny, layers, seg_rows), out_s...  57.6 us
    unnamed x4, local copies, waits for them, and re-layouts  2.22 us

profile of v4, /device:TPU:0, one launch (start us, length us, event | category | flops | bytes accessed | tf_op | source)
XLA Modules:
  0.0 60.5 jit_solution(4791144292949426007)
XLA Ops:
  0.6 57.6 %sweeps.1 = (f32[3,20,8,128]{3,2,1,0:T(8,128)}, f32[2,128]{1,0:T(2,128)}) custom-call(f32[3,20,8,128]{3,2,1,0:T(8,128)} %rhs_h.1, bf16[9,20,8,128]{3,2,1,0:T(8,128)(2,1)} %diag_h.1, bf16[9,20,8,128]{3,2,1,0:T(8,128)(2,1)} %mob_h.1, bf16[3,20,8,128]{3,2,1,0:T(8,128)(2,1)} %trans_h.1, s32[1,8,32]{2,1,0:T(8,128)} %cell_h.1, f32[1,8,32]{2,1,0:T(8,128)} %pi_h.1, ...), custom_call_target="tpu_custom_call" | custom-call | tf_op jit(solution)/shard_map/sweeps/pallas_call | solution.py:456
  58.2 0.0 copy-start
  58.3 1.7 %copy.14 = f32[3,20,8,128]{3,2,1,0:T(8,128)} copy(f32[3,20,8,128]{3,2,1,0:T(8,128)} %get-tuple-element.8) | data formatting | bytes 491520
  59.9 0.0 copy-done
  59.9 0.6 copy.15
Async XLA Ops:
  58.2 1.7 %copy-start = (f32[2,128]{1,0:T(2,128)S(1)}, f32[2,128]{1,0:T(2,128)}, u32[]{:S(2)}) copy-start(f32[2,128]{1,0:T(2,128)} %get-tuple-element.5) | copy-start | bytes 3076

commit v5 on v4

--- a/solution.py
+++ b/solution.py
@@ -218,9 +218,16 @@
     flow[...] = jnp.zeros_like(flow)
 
     def pick_rows(source, target):
-        for o in range(n):
-            at = lax.div(cell_s[0, 0, o], LANE)
-            target[o:o + 1, :] = source[0, pl.ds(at, 1), :]
+        tiles = []
+        for first in range(0, n, SUB):
+            tile = jnp.zeros((SUB, LANE), F32)
+            for o in range(SUB):
+                at = lax.shift_right_logical(cell_s[0, 0, first + o], LANE.bit_length() - 1)
+                one = jnp.broadcast_to(source[0, pl.ds(at, 1), :], (SUB, LANE))
+                tile = jnp.where(row == o, one, tile)
+            tiles.append(tile)
+        for i, tile in enumerate(tiles):
+            target[i * SUB:(i + 1) * SUB, :] = tile
 
     pick_rows(kk, k_rows)
     pick_rows(v, rows)
@@ -385,8 +392,7 @@
         inside()
         borders(slot, last)
 
-    def sweep(k, carry):
-        slot = lax.rem(k, 2)
+    def sweep(k, slot):
         exchange(k, slot, False)
         pick_rows(v, rows)
         came = receive(slot)
@@ -396,11 +402,16 @@
             sums[1:2, :] = jnp.broadcast_to(ratio(came), (1, LANE))
 
         seg[4] = seg[4] + seg[5] / seg[2]
+
+    def two_sweeps(pair, carry):
+        sweep(2 * pair + 1, 1)
+        sweep(2 * pair + 2, 0)
         return carry
 
     last = 2 * SWEEPS
-    lax.fori_loop(1, last, sweep, 0)
-    slot = last % 2
+    lax.fori_loop(0, SWEEPS - 1, two_sweeps, 0)
+    sweep(last - 1, 1)
+    slot = 0
     omega = sums[1:2, :]
     exchange(last, slot, True)
     receive(slot)

time: 60.7 us -> 60.6 us (level)
  no operation moved by 1% of the time
where the time goes in v5:
time: 60.6 us; the launch traced here: 60.4 us
  Pallas kernels  57.5 us (95%)
  local copies, waits for them, and re-layouts  2.22 us (4%)
  between operations  0.65 us (1%)
    pallas_call x1, Pallas kernels, on_device(): pl.pallas_call(functools.partial(kernel, nx, ny, layers, seg_rows), out_s...  57.5 us
    unnamed x4, local copies, waits for them, and re-layouts  2.22 us

profile of v5, /device:TPU:0, one launch (start us, length us, event | category | flops | bytes accessed | tf_op | source)
XLA Modules:
  0.0 60.4 jit_solution(2411029367511113421)
XLA Ops:
  0.6 57.5 %sweeps.1 = (f32[3,20,8,128]{3,2,1,0:T(8,128)}, f32[2,128]{1,0:T(2,128)}) custom-call(f32[3,20,8,128]{3,2,1,0:T(8,128)} %rhs_h.1, bf16[9,20,8,128]{3,2,1,0:T(8,128)(2,1)} %diag_h.1, bf16[9,20,8,128]{3,2,1,0:T(8,128)(2,1)} %mob_h.1, bf16[3,20,8,128]{3,2,1,0:T(8,128)(2,1)} %trans_h.1, s32[1,8,32]{2,1,0:T(8,128)} %cell_h.1, f32[1,8,32]{2,1,0:T(8,128)} %pi_h.1, ...), custom_call_target="tpu_custom_call" | custom-call | tf_op jit(solution)/shard_map/sweeps/pallas_call | solution.py:467
  58.1 0.0 copy-start
  58.1 1.7 %copy.14 = f32[3,20,8,128]{3,2,1,0:T(8,128)} copy(f32[3,20,8,128]{3,2,1,0:T(8,128)} %get-tuple-element.8) | data formatting | bytes 491520
  59.8 0.0 copy-done
  59.8 0.6 copy.15
Async XLA Ops:
  58.1 1.7 %copy-start = (f32[2,128]{1,0:T(2,128)S(1)}, f32[2,128]{1,0:T(2,128)}, u32[]{:S(2)}) copy-start(f32[2,128]{1,0:T(2,128)} %get-tuple-element.5) | copy-start | bytes 3076

commit v6 on v5

--- a/solution.py
+++ b/solution.py
@@ -99,8 +99,8 @@
             pl.when(come)(copy.wait_recv)
             pl.when(to)(copy.wait_send)
 
-    def send_rows(slot):
-        for target in partners:
+    def send_rows(slot, some=slice(None)):
+        for target in partners[some]:
             pos = target[0] * ny + target[1]
             pltpu.make_async_remote_copy(
                 src_ref=send.at[slot, pl.ds(pos, 1), :], dst_ref=recv.at[slot, pl.ds(me, 1), :],
@@ -169,6 +169,7 @@
 
     zc = 4 if layers % 4 == 0 else 1
     chunks = [slice(z, z + zc) for z in range(0, layers, zc)]
+    few = n // (2 * len(chunks))
     lane = lax.broadcasted_iota(jnp.int32, (SUB, LANE), 1)
     row = lax.broadcasted_iota(jnp.int32, (SUB, LANE), 0)
     edge = (lane == 0) | (lane == LANE - 1)
@@ -292,6 +293,7 @@
                 for c in range(3)
             ]
             packed = publish(zs, vec, packed)
+            send_rows(slot, slice(zs.start // zc * few, (zs.start // zc + 1) * few))
         ypack[slot] = packed
 
     def inside():
@@ -386,7 +388,7 @@
         fill(slot)
         advance(slot)
         send_halos(slot)
-        send_rows(slot)
+        send_rows(slot, slice(len(chunks) * few, None))
         pl.when(k == SWEEPS)(keep_state)
         pl.when(k == SWEEPS + 1)(keep_residual)
         inside()

time: 60.6 us -> 60.6 us (level)
  no operation moved by 1% of the time
where the time goes in v6:
time: 60.6 us; the launch traced here: 60.4 us
  Pallas kernels  57.6 us (95%)
  local copies, waits for them, and re-layouts  2.22 us (4%)
  between operations  0.65 us (1%)
    pallas_call x1, Pallas kernels, on_device(): pl.pallas_call(functools.partial(kernel, nx, ny, layers, seg_rows), out_s...  57.6 us
    unnamed x4, local copies, waits for them, and re-layouts  2.22 us

profile of v6, /device:TPU:0, one launch (start us, length us, event | category | flops | bytes accessed | tf_op | source)
XLA Modules:
  0.0 60.4 jit_solution(3325120818550731191)
XLA Ops:
  0.6 57.6 %sweeps.1 = (f32[3,20,8,128]{3,2,1,0:T(8,128)}, f32[2,128]{1,0:T(2,128)}) custom-call(f32[3,20,8,128]{3,2,1,0:T(8,128)} %rhs_h.1, bf16[9,20,8,128]{3,2,1,0:T(8,128)(2,1)} %diag_h.1, bf16[9,20,8,128]{3,2,1,0:T(8,128)(2,1)} %mob_h.1, bf16[3,20,8,128]{3,2,1,0:T(8,128)(2,1)} %trans_h.1, s32[1,8,32]{2,1,0:T(8,128)} %cell_h.1, f32[1,8,32]{2,1,0:T(8,128)} %pi_h.1, ...), custom_call_target="tpu_custom_call" | custom-call | tf_op jit(solution)/shard_map/sweeps/pallas_call | solution.py:469
  58.2 0.0 copy-start
  58.2 1.7 %copy.14 = f32[3,20,8,128]{3,2,1,0:T(8,128)} copy(f32[3,20,8,128]{3,2,1,0:T(8,128)} %get-tuple-element.8) | data formatting | bytes 491520
  59.9 0.0 copy-done
  59.9 0.6 copy.15
Async XLA Ops:
  58.2 1.7 %copy-start = (f32[2,128]{1,0:T(2,128)S(1)}, f32[2,128]{1,0:T(2,128)}, u32[]{:S(2)}) copy-start(f32[2,128]{1,0:T(2,128)} %get-tuple-element.5) | copy-start | bytes 3076
